TPU v7x, 512 devices: a whole 4x4x16 slice. The times are simulated.
512 devices in a mesh: grp: 4 (over z_hi), dp: 8 (over z_lo, core), tp: 16 (over x, y).
Axes of the slice: x: 4, y: 4, z: 16 (z_hi: 4, z_lo: 4; z = z_hi * 4 + z_lo), core: 2. Of those that a mesh axis runs over, the one named last changes fastest.
Arguments:
- grad_partials: bfloat16 [8, 16384, 4096], P('dp', 'tp', 'grp'), may hold values from -6 to 6
- master: float32 [16384, 4096], P('tp', ('grp', 'dp')), may hold values from -0.046875 to 0.046875
- moment: float32 [16384, 4096], P('tp', ('grp', 'dp')), may hold values from -3 to 3
- second: float32 [16384, 4096], P('tp', ('grp', 'dp')), may hold values from 0.25 to 4
- state: bfloat16 [1024, 4096], P(('grp', 'dp'), 'tp'), may hold values from -6 to 6
- hidden: bfloat16 [4, 1024, 16384], P(None, ('grp', 'dp'), 'tp'), may hold values from -6 to 6
- queries: bfloat16 [4, 1024, 4096], P(None, ('grp', 'dp'), 'tp'), may hold values from -6 to 6
- fresh_kv: bfloat16 [4, 1024, 2, 512], P(None, ('grp', 'dp'), None, 'tp'), may hold values from -4 to 4
- cache_k: bfloat16 [1024, 128, 128], P(('grp', 'dp'), 'tp'), may hold values from -4 to 4
- cache_v: bfloat16 [1024, 128, 128], P(('grp', 'dp'), 'tp'), may hold values from -4 to 4
- cache_scale: bfloat16 [1024, 2, 128], P(('grp', 'dp'), None, 'tp'), may hold values from 0.25 to 256, as said below
- lengths: int32 [1024], P(('grp', 'dp')), may hold values from 16 to 128, as said below
Outputs:
- codes: bfloat16 [16384, 4096], P('tp', ('grp', 'dp'))
- state_out: bfloat16 [1024, 4096], P(('grp', 'dp'), 'tp')
Inputs may be any that keep to these rules, and one draw needn't show every extreme that they name: `lengths`: 16 or more for every row; in every draw some row has exactly 16 and some row exactly 128. `cache_scale`: positive.
All inputs are finite; a program needn't handle non-finite values.
Results may differ from a plain program's by a relative error of at most 0.017.
Values may be sent and summed in bfloat16 or wider, within the bound.
No kernel may reach another device: no remote copies, remote signals or barrier semaphores. Data moves between devices by JAX's collectives and lax.ppermute only.
A program may use at most 64 MiB of HBM per device.

v0:
```python
import math

import jax
import jax.numpy as jnp
from jax import lax
from jax.sharding import PartitionSpec as P

HD = 128
KVH = 4
BLK = 128
CACHE = 32
SINK = 4
STEPS = 4


beta_first = 0.9
beta_second = 0.95
adam_eps = 1e-08
weight_decay = 0.1
learn_rate = 0.01
adam_count = 100.0
scale_eps = 1e-06


def partner_2(value, axis, distance):
    mask = 2**distance
    pairs = [(source, source ^ mask) for source in range(lax.axis_size(axis))]
    return lax.ppermute(value, axis, pairs)


def adamw_update(master, moment, second, grad):
    moment_new = beta_first * moment + (1.0 - beta_first) * grad
    second_new = beta_second * second + (1.0 - beta_second) * grad * grad
    moment_hat = moment_new / (1.0 - beta_first**adam_count)
    second_hat = second_new / (1.0 - beta_second**adam_count)
    return master - learn_rate * (
        moment_hat / (jnp.sqrt(second_hat) + adam_eps) + weight_decay * master
    )


def quantize_blocks(weight, block):
    nrow, ncol = weight.shape
    tiles = weight.reshape(nrow // block, block, ncol // block, block)
    peak = jnp.max(jnp.abs(tiles), axis=(1, 3))
    scale = (peak + scale_eps).astype(jnp.bfloat16)
    codes = (tiles / scale.astype(jnp.float32)[:, None, :, None]).astype(jnp.bfloat16)
    return (codes.reshape(nrow, ncol), scale)


def slot_mask(lengths, step, cache_len, sink):
    window = cache_len - sink
    slots = jnp.arange(cache_len, dtype=jnp.int32)
    keep = slots[None, :] < lengths[:, None]
    for done in range(step + 1):
        evicted = sink + (lengths + done - sink) % window
        keep = keep & (slots[None, :] != evicted[:, None])
    return keep


def attend(query, cache_k, cache_v, cache_scale, keep, new_keys, new_values, step):
    nrow, groups, heads, head = query.shape
    inv = 1.0 / math.sqrt(head)
    seen = jnp.arange(new_keys.shape[2], dtype=jnp.int32) <= step
    old = jnp.einsum("rgqh,rgjh->rgqj", query, cache_k, preferred_element_type=jnp.float32) * (
        cache_scale[:, :, 0, None, :] * inv
    )
    old = jnp.where(keep[:, None, None, :], old, -jnp.inf)
    fresh = jnp.einsum("rgqh,rgsh->rgqs", query, new_keys, preferred_element_type=jnp.float32) * inv
    fresh = jnp.where(seen[None, None, None, :], fresh, -jnp.inf)
    top = jnp.maximum(jnp.max(old, axis=-1), jnp.max(fresh, axis=-1))[..., None]
    old_w = jnp.exp(old - top)
    fresh_w = jnp.exp(fresh - top)
    total = jnp.sum(old_w, axis=-1, keepdims=True) + jnp.sum(fresh_w, axis=-1, keepdims=True)
    old_p = (old_w / total * cache_scale[:, :, 1, None, :]).astype(jnp.bfloat16)
    fresh_p = (fresh_w / total).astype(jnp.bfloat16)
    out = jnp.einsum("rgqj,rgjh->rgqh", old_p, cache_v, preferred_element_type=jnp.float32)
    out = out + jnp.einsum(
        "rgqs,rgsh->rgqh", fresh_p, new_values, preferred_element_type=jnp.float32
    )
    return out.reshape(nrow, groups * heads * head)


def block_product(rows_hidden, codes, scale_cols):
    nblock = codes.shape[0] // BLK
    split_hidden = rows_hidden.reshape(rows_hidden.shape[0], nblock, BLK)
    split_codes = codes.reshape(nblock, BLK, codes.shape[1])
    parts = jnp.einsum(
        "rbi,bic->brc", split_hidden, split_codes, preferred_element_type=jnp.float32
    )
    return jnp.sum(parts * scale_cols[:, None, :], axis=0)


def share_heads(cache_k, cache_v, cache_scale, fresh_rows):
    tp_count = lax.axis_size("tp")
    group_size = max(1, tp_count // KVH)
    pieces = [cache_k, cache_v, cache_scale, fresh_rows]
    join_axes = [1, 1, 2, 3]
    for bit in range(group_size.bit_length() - 1):
        nrow = pieces[0].shape[0]
        widths = [piece.size // nrow for piece in pieces]
        packed = jnp.concatenate([piece.reshape(nrow, -1) for piece in pieces], axis=1)
        partner = partner_2(packed, "tp", bit)
        upper_half = lax.axis_index("tp") // (1 << bit) % 2 == 1
        joined = []
        offset = 0
        for piece, width, axis_join in zip(pieces, widths, join_axes):
            theirs = partner[:, offset : offset + width].reshape(piece.shape)
            offset = offset + width
            lower = jnp.where(upper_half, theirs, piece)
            higher = jnp.where(upper_half, piece, theirs)
            joined.append(jnp.concatenate([lower, higher], axis=axis_join))
        pieces = joined
    return pieces


def shards(
    grad_partials,
    master,
    moment,
    second,
    state,
    hidden,
    queries,
    fresh_kv,
    cache_k,
    cache_v,
    cache_scale,
    lengths,
):
    summed = lax.psum_scatter(grad_partials, "dp", scatter_dimension=2, tiled=True).astype(
        jnp.float32
    )[0]
    weight = adamw_update(master, moment, second, summed)
    codes, scale = quantize_blocks(weight, BLK)
    whole_codes, whole_scale = (
        lax.all_gather(codes, ("grp", "dp"), axis=1, tiled=True),
        lax.all_gather(scale, ("grp", "dp"), axis=1, tiled=True),
    )
    whole_cols = jnp.repeat(whole_scale.astype(jnp.float32), BLK, axis=1)
    feat = state.shape[1]
    nrow = state.shape[0]
    heads_here = max(1, KVH // lax.axis_size("tp"))
    fresh_rows = fresh_kv.transpose(1, 0, 2, 3)
    keys_all, values_all, scales_all, fresh_all = share_heads(
        cache_k, cache_v, cache_scale, fresh_rows
    )
    keys_all = keys_all.reshape(nrow, heads_here, CACHE, HD)
    values_all = values_all.reshape(nrow, heads_here, CACHE, HD)
    scales_all = (
        scales_all.astype(jnp.float32).reshape(nrow, 2, heads_here, CACHE).transpose(0, 2, 1, 3)
    )
    fresh_all = fresh_all.reshape(nrow, STEPS, 2, heads_here, HD)
    new_keys = fresh_all[:, :, 0].transpose(0, 2, 1, 3)
    new_values = fresh_all[:, :, 1].transpose(0, 2, 1, 3)
    for step in range(STEPS):
        query = queries[step].reshape(nrow, heads_here, -1, HD)
        keep = slot_mask(lengths, step, CACHE, SINK)
        attention = attend(
            query, keys_all, values_all, scales_all, keep, new_keys, new_values, step
        )
        total = lax.psum(block_product(hidden[step], whole_codes, whole_cols), "tp")
        mixed = lax.dynamic_slice_in_dim(total, lax.axis_index("tp") * feat, feat, 1)
        state = (state.astype(jnp.float32) + attention + mixed).astype(jnp.bfloat16)
    return (codes, state)


def solution(mesh):
    return jax.shard_map(
        shards,
        mesh=mesh,
        in_specs=(
            P("dp", "tp", "grp"),
            P("tp", ("grp", "dp")),
            P("tp", ("grp", "dp")),
            P("tp", ("grp", "dp")),
            P(("grp", "dp"), "tp"),
            P(None, ("grp", "dp"), "tp"),
            P(None, ("grp", "dp"), "tp"),
            P(None, ("grp", "dp"), None, "tp"),
            P(("grp", "dp"), "tp", None),
            P(("grp", "dp"), "tp", None),
            P(("grp", "dp"), None, "tp"),
            P(("grp", "dp")),
        ),
        out_specs=(P("tp", ("grp", "dp")), P(("grp", "dp"), "tp")),
        check_vma=False,
    )
```

profile of v0, /device:TPU:1, one launch (start us, length us, event | category | flops | bytes accessed | tf_op | source)
XLA Modules:
  0.0 310.1 jit_solution(16302182319325970237)
XLA Ops:
  7.2 10.8 %copy.72 = bf16[1,1024,1024]{1,0,2:T(2,128)(2,1)} copy(bf16[1,1024,1024]{2,1,0:T(8,128)(2,1)} %param.12) | data formatting | bytes 4194304
  18.0 4.4 %copy.129 = bf16[1024,1,1024]{2,0,1:T(8,128)(2,1)} copy(bf16[1024,1,1024]{2,1,0:T(2,128)(2,1)} %bitcast.191) | data formatting | bytes 4194304
  22.6 49.1 %reduce-scatter.4.cloned.1.call-done = bf16[128,1024]{1,0:T(8,128)(2,1)} async-done(((bf16[1024,1024]{1,0:T(8,128)(2,1)}), bf16[128,1024]{1,0:T(8,128)(2,1)}) %reduce-scatter.4.cloned.1.call-update) | async-done | bytes 262160
  71.7 1.2 reshape_bitcast_fusion
  73.0 0.4 copy.73
  73.4 0.5 abs_reduce_fusion
  74.2 0.9 divide_convert_fusion
  75.6 3.0 collective-permute-start
  78.9 2.7 collective-permute-done
  82.8 4.3 %collective-permute-start.1 = (bf16[32,4640]{1,0:T(8,128)(2,1)S(1)}, bf16[32,4640]{1,0:T(8,128)(2,1)S(1)}, u32[]{:S(2)}, u32[]{:S(2)}) collective-permute-start(bf16[32,4640]{1,0:T(8,128)(2,1)S(1)} %concatenate.58), channel_id=1, source_target_pairs={{0,2},{1,3},{2,0},{3,1},{4,6},{5,7},{6,4},{7,5},{8,10},{9,11},{10,... | collective-permute-start | bytes 890888 | tf_op jit(solution)/shard_map/ppermute | solution.py:28
  87.3 4.6 %collective-permute-done.1 = bf16[32,4640]{1,0:T(8,128)(2,1)S(1)} collective-permute-done((bf16[32,4640]{1,0:T(8,128)(2,1)S(1)}, bf16[32,4640]{1,0:T(8,128)(2,1)S(1)}, u32[]{:S(2)}, u32[]{:S(2)}) %collective-permute-start.1) | collective-permute-done | bytes 296992 | tf_op jit(solution)/shard_map/ppermute | solution.py:28
  92.7 0.3 fusion.89
  93.3 0.3 fusion.87
  93.8 0.3 fusion.91
  94.4 0.3 fusion.85
  96.4 34.7 %all-gather = bf16[32,1,8]{2,1,0:T(2,128)(2,1)S(1)} all-gather(bf16[1,1,8]{2,1,0:T(2,128)(2,1)S(1)} %get-tuple-element.42), channel_id=1, replica_groups=mesh['grp'=4,'dp'=8,'tp'=16] {'grp','dp'}, dimensions={0}, use_global_device_ids=true | all-gather | bytes 528 | tf_op jit(solution)/shard_map/all_gather | solution.py:137
  131.1 42.9 %all-gather.3.cloned.1.call-done = bf16[1024,4096]{1,0:T(8,128)(2,1)} async-done(((bf16[1024,128]{1,0:T(8,128)(2,1)}), bf16[1024,4096]{1,0:T(8,128)(2,1)}) %all-gather.3.cloned.1.call-update) | async-done | bytes 8388624 | tf_op jit(solution)/shard_map/all_gather | solution.py:136
  174.1 5.6 %fusion.1 = f32[4096,32]{0,1:T(8,128)} fusion(f32[8,4096]{1,0:T(8,128)S(1)} %broadcast_bitcast_fusion, bf16[8,128,4096]{2,1,0:T(8,128)(2,1)} %bitcast.187, bf16[32,8,128]{2,1,0:T(8,128)(2,1)S(1)} %bitcast.203), kind=kOutput, calls=%fused_computation.6 | convolution fusion | flops 270401536 | bytes 9109504 | tf_op jit(solution)/shard_map/rbi,bic->brc/dot_general | solution.py:87
  179.8 2.1 fusion.2
  181.9 2.0 fusion.3
  183.9 2.0 fusion
  187.4 0.3 convolution_add_fusion.2
  188.5 113.6 %all-reduce.3.cloned.1.call-done = (f32[32,4096]{1,0:T(8,128)}, f32[32,4096]{1,0:T(8,128)}, f32[32,4096]{1,0:T(8,128)}, f32[32,4096]{1,0:T(8,128)}) async-done(((f32[32,4096]{1,0:T(8,128)}, f32[32,4096]{1,0:T(8,128)}, f32[32,4096]{1,0:T(8,128)}, f32[32,4096]{1,0:T(8,128)}), (f32[32,4096]{1,0:T(8,128)}, f32[32,4096]{1,0:T(8,128)}, f32[32,4096]{1,0:T(8,128)}, ...) | async-done | bytes 2097168 | tf_op jit(solution)/shard_map/psum | solution.py:161
  302.1 1.4 fusion.35
  (121 shorter events, 7.6 us)
Async XLA Ops:
  7.2 64.6 %reduce-scatter.4.cloned.1.call-start = ((), (), s32[]{:S(2)}) async-start(), calls=%async_computation.2 | async-start | bytes 2359296
  18.0 55.4 %copy-start.1 = (f32[1024,128]{1,0:T(8,128)S(1)}, f32[1024,128]{1,0:T(8,128)}, u32[]{:S(2)}) copy-start(f32[1024,128]{1,0:T(8,128)} %param.13) | copy-start | bytes 1572868
  18.0 55.4 %copy-start.2 = (f32[1024,128]{1,0:T(8,128)S(1)}, f32[1024,128]{1,0:T(8,128)}, u32[]{:S(2)}) copy-start(f32[1024,128]{1,0:T(8,128)} %param.15) | copy-start | bytes 1572868
  18.0 55.4 %copy-start.3 = (f32[1024,128]{1,0:T(8,128)S(1)}, f32[1024,128]{1,0:T(8,128)}, u32[]{:S(2)}) copy-start(f32[1024,128]{1,0:T(8,128)} %param.14) | copy-start | bytes 1572868
  22.5 52.7 %copy-start.10 = (bf16[32,2,8]{0,2,1:T(8,128)(2,1)S(1)}, bf16[32,2,8]{0,2,1:T(8,128)(2,1)}, u32[]{:S(2)}) copy-start(bf16[32,2,8]{0,2,1:T(8,128)(2,1)} %param.22) | copy-start | bytes 3076
  22.5 52.8 %copy-start.5 = (bf16[4,32,2,32]{3,2,1,0:T(2,128)(2,1)S(1)}, bf16[4,32,2,32]{3,2,1,0:T(2,128)(2,1)}, u32[]{:S(2)}) copy-start(bf16[4,32,2,32]{3,2,1,0:T(2,128)(2,1)} %param.19) | copy-start | bytes 49156
  22.5 53.0 %copy-start.6 = (bf16[32,8,128]{2,1,0:T(8,128)(2,1)S(1)}, bf16[32,8,128]{2,1,0:T(8,128)(2,1)}, u32[]{:S(2)}) copy-start(bf16[32,8,128]{2,1,0:T(8,128)(2,1)} %param.21) | copy-start | bytes 196612
  22.5 53.0 %copy-start.7 = (bf16[32,8,128]{2,1,0:T(8,128)(2,1)S(1)}, bf16[32,8,128]{2,1,0:T(8,128)(2,1)}, u32[]{:S(2)}) copy-start(bf16[32,8,128]{2,1,0:T(8,128)(2,1)} %param.20) | copy-start | bytes 196612
  22.5 56.1 %copy-start.11 = (s32[32]{0:T(128)S(1)}, s32[32]{0:T(128)}, u32[]{:S(2)}) copy-start(s32[32]{0:T(128)} %param.23) | copy-start | bytes 388
  22.5 56.2 %copy-start.8 = (bf16[4,32,256]{2,1,0:T(8,128)(2,1)S(1)}, bf16[4,32,256]{2,1,0:T(8,128)(2,1)}, u32[]{:S(2)}) copy-start(bf16[4,32,256]{2,1,0:T(8,128)(2,1)} %param.18) | copy-start | bytes 196612
  22.5 56.2 %copy-start.4 = (bf16[4,32,1024]{2,1,0:T(8,128)(2,1)S(1)}, bf16[4,32,1024]{2,1,0:T(8,128)(2,1)}, u32[]{:S(2)}) copy-start(bf16[4,32,1024]{2,1,0:T(8,128)(2,1)} %param.17) | copy-start | bytes 786436
  22.6 151.5 %all-gather.3.cloned.1.call-start = ((), (), s32[]{:S(2)}) async-start(), calls=%async_computation.1 | async-start | bytes 8650752 | tf_op jit(solution)/shard_map/all_gather | solution.py:136
  75.1 227.0 %all-reduce.3.cloned.1.call-start = ((), (), s32[]{:S(2)}) async-start(), calls=%async_computation.3 | async-start | bytes 4194304 | tf_op jit(solution)/shard_map/psum | solution.py:161
  75.6 6.0 %collective-permute-start = (bf16[32,2320]{1,0:T(8,128)(2,1)S(1)}, bf16[32,2320]{1,0:T(8,128)(2,1)S(1)}, u32[]{:S(2)}, u32[]{:S(2)}) collective-permute-start(bf16[32,2320]{1,0:T(8,128)(2,1)S(1)} %concatenate.53), channel_id=1, source_target_pairs={{0,1},{1,0},{2,3},{3,2},{4,5},{5,4},{6,7},{7,6},{8,9},{9,8},{10,11... | collective-permute-start | bytes 445448 | tf_op jit(solution)/shard_map/ppermute | solution.py:28
  82.8 9.1 %collective-permute-start.1 = (bf16[32,4640]{1,0:T(8,128)(2,1)S(1)}, bf16[32,4640]{1,0:T(8,128)(2,1)S(1)}, u32[]{:S(2)}, u32[]{:S(2)}) collective-permute-start(bf16[32,4640]{1,0:T(8,128)(2,1)S(1)} %concatenate.58), channel_id=1, source_target_pairs={{0,2},{1,3},{2,0},{3,1},{4,6},{5,7},{6,4},{7,5},{8,10},{9,11},{10,... | collective-permute-start | bytes 890888 | tf_op jit(solution)/shard_map/ppermute | solution.py:28
  174.1 5.8 %copy-start = (bf16[1024,4096]{1,0:T(8,128)(2,1)S(1)}, bf16[1024,4096]{1,0:T(8,128)(2,1)}, u32[]{:S(2)}) copy-start(bf16[1024,4096]{1,0:T(8,128)(2,1)} %all-gather.3.cloned.1.call-done) | copy-start | bytes 25165828
  186.0 116.2 %copy-start.9 = (bf16[32,256]{1,0:T(8,128)(2,1)S(1)}, bf16[32,256]{1,0:T(8,128)(2,1)}, u32[]{:S(2)}) copy-start(bf16[32,256]{1,0:T(8,128)(2,1)} %param.16) | copy-start | bytes 49156
Sparse Core Ops, SparseCore 0:
  22.7 49.0 reduce-scatter.3
  75.2 98.7 all-gather.2
  186.1 115.9 all-reduce.2
where the time goes:
time: 311 us; the launch traced here: 310 us
  waiting for transfers between devices  213 us (68%)
  blocking collectives  34.7 us (11%)
  local copies, waits for them, and re-layouts  19.1 us (6%)
  matrix products  16.1 us (5%)
  between operations  14.4 us (5%)
  starting transfers between devices  7.43 us (2%)
  other arithmetic  5.44 us (2%)
    psum x1, waiting for transfers between devices, shards(): total = lax.psum(block_product(hidden[step], whole_codes, whole_cols), 'tp')  114 us
    unnamed x4, waiting for transfers between devices  49.2 us
    all_gather x1, waiting for transfers between devices, shards(): lax.all_gather(codes, ('grp', 'dp'), axis=1, tiled=True)  42.9 us
    all_gather x1, blocking collectives, shards(): lax.all_gather(scale, ('grp', 'dp'), axis=1, tiled=True)  34.7 us
    unnamed x42, local copies, waits for them, and re-layouts  17.4 us
    dot_general x4, matrix products, block_product(): jnp.einsum('rbi,bic->brc', split_hidden, split_codes, preferred_element_t...  11.8 us
    ppermute x2, starting transfers between devices, partner_2(): return lax.ppermute(value, axis, pairs)  7.31 us
    ppermute x2, waiting for transfers between devices, partner_2(): return lax.ppermute(value, axis, pairs)  7.28 us
  transfers between devices with their start and end apart: 5, of which 5 were waited for; matrix products, arithmetic and copies ran while one was open for 3% of the time, Pallas kernels for 0%

commit v1 on v0

v1 whole, which is shorter than its diff:
```python
import math

import jax
import jax.numpy as jnp
import numpy as np
from jax import lax
from jax.experimental import pallas as pl
from jax.experimental.pallas import tpu as pltpu
from jax.sharding import PartitionSpec as P

HD = 128
BLK = 128
CACHE = 32
SINK = 4
STEPS = 4
QUADS = 4
CHIPS = 16
ROWS = 32
UNITS = 1024
SLOTS = CACHE // QUADS

beta_first = 0.9
beta_second = 0.95
adam_eps = 1e-08
weight_decay = 0.1
learn_rate = 0.01
adam_count = 100.0
scale_eps = 1e-06

Z = ("grp", "dp")
ALL = ("grp", "dp", "tp")
F32 = jnp.float32
BF16 = jnp.bfloat16
VMEM_LIMIT = 48 * 1024 * 1024


def params():
    return pltpu.CompilerParams(vmem_limit_bytes=VMEM_LIMIT)


def ring_distance(a, b, n):
    d = abs(a - b) % n
    return min(d, n - d)


def row_places():
    places = []
    for c in range(CHIPS):
        by_z = sorted(range(CHIPS), key=lambda r: (-ring_distance(c, r, CHIPS), r))
        by_xy = sorted(
            range(CHIPS),
            key=lambda p: (ring_distance(p // 4, c // 4, 4) + ring_distance(p % 4, c % 4, 4), p),
        )
        place = [0] * CHIPS
        for r, p in zip(by_z, by_xy):
            place[r] = p
        places.append(place)
    return places


PLACES = row_places()
ROW_AT = np.argsort(np.array(PLACES), axis=1).astype(np.int32)


def home_pairs():
    return [
        ((c * 2 + b) * CHIPS + PLACES[c][r], (r * 2 + b) * CHIPS + c)
        for c in range(CHIPS)
        for b in range(2)
        for r in range(CHIPS)
    ]


def flip(value, mask):
    return lax.ppermute(value, "dp", [(s, s ^ mask) for s in range(8)])


def split_kernel(index_ref, grad_ref, out_ref):
    out_ref[0] = grad_ref[...]


def take_chunks(index, grad):
    return pl.pallas_call(
        split_kernel,
        grid_spec=pltpu.PrefetchScalarGridSpec(
            num_scalar_prefetch=1,
            grid=(4,),
            in_specs=[pl.BlockSpec((UNITS, BLK), lambda j, index: (0, index[j]))],
            out_specs=pl.BlockSpec((1, UNITS, BLK), lambda j, index: (j, 0, 0)),
        ),
        out_shape=jax.ShapeDtypeStruct((4, UNITS, BLK), BF16),
        compiler_params=params(),
        name="take_chunks",
    )(index, grad)


def core_sum_kernel(index_ref, near_ref, far_ref, near_in_ref, far_in_ref, keep_ref, send_ref):
    keep_ref[0] = (near_ref[...].astype(F32) + near_in_ref[0].astype(F32)).astype(BF16)
    send_ref[0] = (far_ref[...].astype(F32) + far_in_ref[0].astype(F32)).astype(BF16)


def core_sum(index, grad, received):
    whole = lambda shift: pl.BlockSpec((UNITS, BLK), lambda j, index: (0, index[j + shift]))
    part = lambda shift: pl.BlockSpec((1, UNITS, BLK), lambda j, index: (j + shift, 0, 0))
    shape = jax.ShapeDtypeStruct((2, UNITS, BLK), BF16)
    return pl.pallas_call(
        core_sum_kernel,
        grid_spec=pltpu.PrefetchScalarGridSpec(
            num_scalar_prefetch=1,
            grid=(2,),
            in_specs=[whole(0), whole(2), part(0), part(2)],
            out_specs=[part(0), part(0)],
        ),
        out_shape=[shape, shape],
        compiler_params=params(),
        name="core_sum",
    )(index, grad, grad, received, received)


def pair_sum_kernel(keep_ref, received_ref, out_ref):
    out_ref[...] = (keep_ref[0].astype(F32) + received_ref[0].astype(F32)).astype(BF16)


def pair_sum(keep, received):
    spec = pl.BlockSpec((1, UNITS, BLK), lambda i: (1, 0, 0))
    return pl.pallas_call(
        pair_sum_kernel,
        grid=(1,),
        in_specs=[spec, spec],
        out_specs=pl.BlockSpec((UNITS, BLK), lambda i: (0, 0)),
        out_shape=jax.ShapeDtypeStruct((UNITS, BLK), BF16),
        compiler_params=params(),
        name="pair_sum",
    )(keep, received)


def update_kernel(
    keep_ref, second_in_ref, third_in_ref, master_ref, moment_ref, second_ref, codes_ref, packed_ref
):
    for block in range(UNITS // BLK):
        rows = slice(block * BLK, (block + 1) * BLK)
        grad = (
            keep_ref[0, rows].astype(F32)
            + second_in_ref[0, rows].astype(F32)
            + third_in_ref[rows].astype(F32)
        )
        master = master_ref[rows]
        moment_new = beta_first * moment_ref[rows] + (1.0 - beta_first) * grad
        second_new = beta_second * second_ref[rows] + (1.0 - beta_second) * grad * grad
        moment_hat = moment_new / (1.0 - beta_first**adam_count)
        second_hat = second_new / (1.0 - beta_second**adam_count)
        weight = master - learn_rate * (
            moment_hat / (jnp.sqrt(second_hat) + adam_eps) + weight_decay * master
        )
        peak = jnp.max(jnp.max(jnp.abs(weight), axis=0, keepdims=True), axis=1, keepdims=True)
        scale = (peak + scale_eps).astype(BF16)
        codes = (weight / scale.astype(F32)).astype(BF16)
        codes_ref[rows] = codes
        packed_ref[rows] = codes
        packed_ref[UNITS + 16 * block : UNITS + 16 * (block + 1)] = jnp.broadcast_to(
            scale, (16, BLK)
        )


PACKED = UNITS + 16 * (UNITS // BLK)


def update(keep, second_in, third_in, master, moment, second):
    first = pl.BlockSpec((1, UNITS, BLK), lambda i: (0, 0, 0))
    flat = pl.BlockSpec((UNITS, BLK), lambda i: (0, 0))
    return pl.pallas_call(
        update_kernel,
        grid=(1,),
        in_specs=[first, first, flat, flat, flat, flat],
        out_specs=[flat, pl.BlockSpec((PACKED, BLK), lambda i: (0, 0))],
        out_shape=[
            jax.ShapeDtypeStruct((UNITS, BLK), BF16),
            jax.ShapeDtypeStruct((PACKED, BLK), BF16),
        ],
        compiler_params=params(),
        name="update",
    )(keep, second_in, third_in, master, moment, second)


def project_kernel(order_ref, near_ref, far_ref, own_ref, other_ref, out_ref, sums):
    half = CHIPS // 2
    core = order_ref[CHIPS]
    for side, rows_ref in enumerate((near_ref, far_ref)):
        for which, codes_ref in enumerate((own_ref, other_ref)):
            total = jnp.zeros((half * ROWS, BLK), F32)
            for block in range(UNITS // BLK):
                rows = rows_ref[:, :, block * BLK : (block + 1) * BLK].reshape(half * ROWS, BLK)
                codes = codes_ref[block * BLK : (block + 1) * BLK]
                scale = codes_ref[UNITS + 16 * block : UNITS + 16 * (block + 1)][:1].astype(F32)
                total = total + jnp.dot(rows, codes, preferred_element_type=F32) * scale
            sums[which, side * half : (side + 1) * half] = total.astype(BF16).reshape(
                half, ROWS, BLK
            )
    for place in range(CHIPS):
        row_block = order_ref[place]
        out_ref[place, core] = sums[0, row_block]
        out_ref[place, 1 - core] = sums[1, row_block]


def project(order, near, far, own, other):
    return pl.pallas_call(
        project_kernel,
        grid_spec=pltpu.PrefetchScalarGridSpec(
            num_scalar_prefetch=1,
            grid=(1,),
            in_specs=[
                pl.BlockSpec((CHIPS // 2, ROWS, UNITS), lambda i, order: (0, 0, 0)),
                pl.BlockSpec((CHIPS // 2, ROWS, UNITS), lambda i, order: (0, 0, 0)),
                pl.BlockSpec((PACKED, BLK), lambda i, order: (0, 0)),
                pl.BlockSpec((PACKED, BLK), lambda i, order: (0, 0)),
            ],
            out_specs=pl.BlockSpec((CHIPS, 2, ROWS, BLK), lambda i, order: (0, 0, 0, 0)),
            scratch_shapes=[pltpu.VMEM((2, CHIPS, ROWS, BLK), BF16)],
        ),
        out_shape=jax.ShapeDtypeStruct((CHIPS, 2, ROWS, BLK), BF16),
        compiler_params=params(),
        name="project",
    )(order, near, far, own, other)


def unit_sum_kernel(parts_ref, out_ref):
    total = parts_ref[0].astype(F32)
    for index in range(1, CHIPS):
        total = total + parts_ref[index].astype(F32)
    out_ref[...] = total.astype(BF16)


def unit_sum(parts):
    return pl.pallas_call(
        unit_sum_kernel,
        out_shape=jax.ShapeDtypeStruct((2, ROWS, BLK), BF16),
        compiler_params=params(),
        name="unit_sum",
    )(parts)


def finish_kernel(state_ref, attention_ref, mixed_ref, out_ref):
    for half in range(2):
        cols = slice(half * BLK, (half + 1) * BLK)
        out_ref[:, cols] = (
            state_ref[:, cols].astype(F32) + attention_ref[:, cols] + mixed_ref[half].astype(F32)
        ).astype(BF16)


def finish(state, attention, mixed):
    return pl.pallas_call(
        finish_kernel,
        out_shape=jax.ShapeDtypeStruct(state.shape, BF16),
        compiler_params=params(),
        name="finish",
    )(state, attention, mixed)


KEYS = ROWS * SLOTS
FRESH = STEPS * ROWS
KV_ROWS = 2 * KEYS + 2 * FRESH + 16


def pack_caches(cache_k, cache_v, cache_scale, fresh_kv, place):
    width = fresh_kv.shape[3]
    fresh = fresh_kv.transpose(2, 0, 1, 3).reshape(2 * FRESH, width)
    lane = lax.broadcasted_iota(jnp.int32, (2 * FRESH, HD), 1)
    fresh = jnp.where(lane // width == place, jnp.tile(fresh, (1, HD // width)), 0)
    scale = cache_scale.transpose(1, 0, 2).reshape(2 * KEYS // HD, HD)
    scale = jnp.pad(scale, ((0, 16 - scale.shape[0]), (0, 0)))
    return jnp.concatenate(
        [cache_k.reshape(KEYS, HD), cache_v.reshape(KEYS, HD), fresh, scale], axis=0
    )


def attend_kernel(marks_ref, queries_ref, packed_ref, out_ref):
    inv = 1.0 / math.sqrt(HD)
    slots = QUADS * KEYS
    keys = packed_ref[:, :KEYS].reshape(slots, HD)
    values = packed_ref[:, KEYS : 2 * KEYS].reshape(slots, HD)
    fresh = packed_ref[0, 2 * KEYS : 2 * KEYS + 2 * FRESH].astype(F32)
    for place in range(1, QUADS):
        fresh = fresh + packed_ref[place, 2 * KEYS : 2 * KEYS + 2 * FRESH].astype(F32)
    fresh = fresh.astype(BF16)
    new_keys, new_values = fresh[:FRESH], fresh[FRESH:]
    scales = packed_ref[:, 2 * KEYS + 2 * FRESH :].astype(F32)
    lines = KEYS // HD
    key_scale = jnp.concatenate(
        [scales[p, i : i + 1] for p in range(QUADS) for i in range(lines)], axis=1
    )
    value_scale = jnp.concatenate(
        [scales[p, lines + i : lines + i + 1] for p in range(QUADS) for i in range(lines)], axis=1
    )
    lane = lax.broadcasted_iota(jnp.int32, (ROWS, slots), 1)
    row = lax.broadcasted_iota(jnp.int32, (ROWS, slots), 0)
    slot = (lane // KEYS) * SLOTS + (lane & (SLOTS - 1))
    live = ((lane // SLOTS) & (ROWS - 1)) == row
    live = live & (slot < marks_ref[:, 0:1])
    new_lane = lax.broadcasted_iota(jnp.int32, (ROWS, FRESH), 1)
    new_row = lax.broadcasted_iota(jnp.int32, (ROWS, FRESH), 0)
    mine = (new_lane & (ROWS - 1)) == new_row
    old_sum = [jnp.zeros((ROWS, slots), F32) for _ in range(2)]
    new_sum = [jnp.zeros((ROWS, FRESH), F32) for _ in range(2)]
    for step in range(STEPS):
        live = live & (slot != marks_ref[:, step + 1 : step + 2])
        seen = mine & (new_lane // ROWS <= step)
        for head in range(2):
            query = queries_ref[step, :, head * HD : (head + 1) * HD]
            across = (((1,), (1,)), ((), ()))
            old = lax.dot_general(query, keys, across, preferred_element_type=F32)
            old = jnp.where(live, old * (key_scale * inv), -jnp.inf)
            new = lax.dot_general(query, new_keys, across, preferred_element_type=F32) * inv
            new = jnp.where(seen, new, -jnp.inf)
            top = jnp.maximum(
                jnp.max(old, axis=1, keepdims=True), jnp.max(new, axis=1, keepdims=True)
            )
            old = jnp.exp(old - top)
            new = jnp.exp(new - top)
            share = 1.0 / (jnp.sum(old, axis=1, keepdims=True) + jnp.sum(new, axis=1, keepdims=True))
            old_sum[head] = old_sum[head] + old * share
            new_sum[head] = new_sum[head] + new * share
    for head in range(2):
        old = (old_sum[head] * value_scale).astype(BF16)
        new = new_sum[head].astype(BF16)
        out_ref[:, head * HD : (head + 1) * HD] = jnp.dot(
            old, values, preferred_element_type=F32
        ) + jnp.dot(new, new_values, preferred_element_type=F32)


def attend(lengths, queries, packed):
    steps = jnp.arange(STEPS, dtype=jnp.int32)
    evicted = SINK + (lengths[:, None] + steps[None, :] - SINK) % (CACHE - SINK)
    marks = jnp.concatenate(
        [lengths[:, None], evicted, jnp.zeros((ROWS, HD - 1 - STEPS), jnp.int32)], axis=1
    )
    return pl.pallas_call(
        attend_kernel,
        out_shape=jax.ShapeDtypeStruct((ROWS, 2 * HD), F32),
        compiler_params=params(),
        name="attend",
    )(marks, queries, packed)


def shards(
    grad_partials,
    master,
    moment,
    second,
    state,
    hidden,
    queries,
    fresh_kv,
    cache_k,
    cache_v,
    cache_scale,
    lengths,
):
    dp = lax.axis_index("dp")
    tp = lax.axis_index("tp")
    core, low = dp % 2, dp // 2
    plane = lax.axis_index("grp") * 4 + low
    grad = grad_partials[0]

    owners = low ^ jnp.array([0, 2, 1, 3], jnp.int32)
    outgoing = take_chunks(2 * owners + 1 - core, grad)
    units = jnp.sum(hidden.astype(F32), axis=0).astype(BF16)
    received = flip(outgoing, 1)
    keep, send = core_sum(2 * owners + core, grad, received)
    second_in = flip(send, 2)

    units, send = lax.optimization_barrier((units, send))
    parity_groups = [
        [g * 8 + (2 * h + l) * 2 + b for g in range(4) for h in range(2)]
        for l in range(2)
        for b in range(2)
    ]
    near = lax.all_gather(units, Z, axis=0, axis_index_groups=parity_groups)

    third = pair_sum(keep, second_in)
    third_in = flip(third, 4)
    far = flip(near, 2)

    caches = pack_caches(cache_k, cache_v, cache_scale, fresh_kv, tp % QUADS)
    caches, _ = lax.optimization_barrier((caches, third))
    quads = [[QUADS * x + y for y in range(QUADS)] for x in range(QUADS)]
    packed = lax.all_gather(caches, "tp", axis=0, axis_index_groups=quads)
    attention = attend(lengths, queries, packed)

    codes, own = update(keep, second_in, third_in, master, moment, second)
    other = flip(own, 1)

    row_at = lax.dynamic_index_in_dim(jnp.array(ROW_AT), plane, 0, keepdims=False)
    order = ((row_at ^ low) & 1) * (CHIPS // 2) + row_at // 2
    order = jnp.concatenate([order, core[None]]).astype(jnp.int32)
    parts = project(order, near, far, own, other)
    parts = lax.all_to_all(parts, "tp", 0, 0)
    mixed = lax.ppermute(unit_sum(parts), ALL, home_pairs())
    return (codes, finish(state, attention, mixed))


def solution(mesh):
    return jax.shard_map(
        shards,
        mesh=mesh,
        in_specs=(
            P("dp", "tp", "grp"),
            P("tp", ("grp", "dp")),
            P("tp", ("grp", "dp")),
            P("tp", ("grp", "dp")),
            P(("grp", "dp"), "tp"),
            P(None, ("grp", "dp"), "tp"),
            P(None, ("grp", "dp"), "tp"),
            P(None, ("grp", "dp"), None, "tp"),
            P(("grp", "dp"), "tp", None),
            P(("grp", "dp"), "tp", None),
            P(("grp", "dp"), None, "tp"),
            P(("grp", "dp")),
        ),
        out_specs=(P("tp", ("grp", "dp")), P(("grp", "dp"), "tp")),
        check_vma=False,
    )
```

time: 311 us -> 125 us (0.40)
  the two profiles are of different devices: /device:TPU:1 before, /device:TPU:32 now
where the time goes in v1:
time: 125 us; the launch traced here: 124 us
  blocking collectives  53.1 us (42%)
  starting transfers between devices  33.5 us (27%)
  waiting for transfers between devices  25.2 us (20%)
  Pallas kernels  7.43 us (6%)
  local copies, waits for them, and re-layouts  2.36 us (2%)
  other arithmetic  1.7 us (1%)
    all_gather x1, blocking collectives, shards(): near = lax.all_gather(units, Z, axis=0, axis_index_groups=parity_groups)  39.4 us
    ppermute x5, starting transfers between devices, flip(): return lax.ppermute(value, 'dp', [(s, s ^ mask) for s in range(8)])  17.9 us
    ppermute x5, waiting for transfers between devices, flip(): return lax.ppermute(value, 'dp', [(s, s ^ mask) for s in range(8)])  17 us
    all_gather x1, blocking collectives, shards(): packed = lax.all_gather(caches, 'tp', axis=0, axis_index_groups=quads)  13.8 us
    ppermute x1, starting transfers between devices, shards(): mixed = lax.ppermute(unit_sum(parts), ALL, home_pairs())  8.68 us
    all_to_all x1, waiting for transfers between devices, shards(): parts = lax.all_to_all(parts, 'tp', 0, 0)  8.18 us
    all_to_all x1, starting transfers between devices, shards(): parts = lax.all_to_all(parts, 'tp', 0, 0)  6.91 us
  transfers between devices with their start and end apart: 7, of which 4 were waited for; matrix products, arithmetic and copies ran while one was open for 1% of the time, Pallas kernels for 2%

profile of v1, /device:TPU:32, one launch (start us, length us, event | category | flops | bytes accessed | tf_op | source)
XLA Modules:
  0.0 124.3 jit_solution(7737580032575006530)
XLA Ops:
  0.6 0.7 add_subtract_fusion
  1.3 1.6 %copy-done = bf16[1,1024,1024]{2,1,0:T(8,128)(2,1)S(1)} copy-done((bf16[1,1024,1024]{2,1,0:T(8,128)(2,1)S(1)}, bf16[1,1024,1024]{2,1,0:T(8,128)(2,1)}, u32[]{:S(2)}) %copy-start) | copy-done | bytes 2097176
  2.9 1.0 take_chunks.1
  3.9 1.9 %collective-permute-start = (bf16[4,1024,128]{2,1,0:T(8,128)(2,1)S(1)}, bf16[4,1024,128]{2,1,0:T(8,128)(2,1)S(1)}, u32[]{:S(2)}, u32[]{:S(2)}) collective-permute-start(bf16[4,1024,128]{2,1,0:T(8,128)(2,1)S(1)} %take_chunks.1), channel_id=1, source_target_pairs={{0,16},{16,0},{32,48},{48,32},{64,80},{80,64},{96,112},{112,96},{1... | collective-permute-start | bytes 3145736 | tf_op jit(solution)/shard_map/ppermute | solution.py:75
  5.9 2.6 %collective-permute-done.near_in_ref.far_in_ref = bf16[4,1024,128]{2,1,0:T(8,128)(2,1)S(1)} collective-permute-done((bf16[4,1024,128]{2,1,0:T(8,128)(2,1)S(1)}, bf16[4,1024,128]{2,1,0:T(8,128)(2,1)S(1)}, u32[]{:S(2)}, u32[]{:S(2)}) %collective-permute-start) | collective-permute-done | bytes 1048608 | tf_op jit(solution)/shard_map/ppermute | solution.py:75
  8.5 1.2 core_sum.1
  9.7 7.5 %collective-permute-start.1 = (bf16[2,1024,128]{2,1,0:T(8,128)(2,1)S(1)}, bf16[2,1024,128]{2,1,0:T(8,128)(2,1)S(1)}, u32[]{:S(2)}, u32[]{:S(2)}) collective-permute-start(bf16[2,1024,128]{2,1,0:T(8,128)(2,1)S(1)} %get-tuple-element.9), channel_id=1, source_target_pairs={{0,32},{16,48},{32,0},{48,16},{64,96},{80,112},{96,64},{112,80},{1... | collective-permute-start | bytes 1572872 | tf_op jit(solution)/shard_map/ppermute | solution.py:75
  17.3 0.1 copy.25
  17.5 0.1 copy.26
  17.9 0.7 fusion.9
  18.6 10.8 %collective-permute-done.1.received_ref.second_in_ref = bf16[2,1024,128]{2,1,0:T(8,128)(2,1)S(1)} collective-permute-done((bf16[2,1024,128]{2,1,0:T(8,128)(2,1)S(1)}, bf16[2,1024,128]{2,1,0:T(8,128)(2,1)S(1)}, u32[]{:S(2)}, u32[]{:S(2)}) %collective-permute-start.1) | collective-permute-done | bytes 524320 | tf_op jit(solution)/shard_map/ppermute | solution.py:75
  29.5 1.9 %collective-permute-start.2 = (bf16[1024,128]{1,0:T(8,128)(2,1)S(1)}, bf16[1024,128]{1,0:T(8,128)(2,1)S(1)}, u32[]{:S(2)}, u32[]{:S(2)}) collective-permute-start(bf16[1024,128]{1,0:T(8,128)(2,1)S(1)} %pair_sum.1), channel_id=1, source_target_pairs={{0,64},{16,80},{32,96},{48,112},{64,0},{80,16},{96,32},{112,48},{1... | collective-permute-start | bytes 786440 | tf_op jit(solution)/shard_map/ppermute | solution.py:75
  31.4 39.4 %all-gather.1 = bf16[256,1024]{1,0:T(8,128)(2,1)S(1)} all-gather(bf16[32,1024]{1,0:T(8,128)(2,1)S(1)} %reduce_sum.12), channel_id=3, replica_groups={{0,64,128,192,256,320,384,448},{16,80,144,208,272,336,400,464},{32,96,1..., dimensions={0}, use_global_device_ids=true | all-gather | bytes 589824 | tf_op jit(solution)/shard_map/all_gather | solution.py:377
  70.8 4.6 %collective-permute-start.3 = (bf16[8,32,1024]{2,1,0:T(8,128)(2,1)S(1)}, bf16[8,32,1024]{2,1,0:T(8,128)(2,1)S(1)}, u32[]{:S(2)}, u32[]{:S(2)}) collective-permute-start(bf16[8,32,1024]{2,1,0:T(8,128)(2,1)S(1)} %bitcast.33), channel_id=1, source_target_pairs={{0,32},{16,48},{32,0},{48,16},{64,96},{80,112},{96,64},{112,80},{1... | collective-permute-start | bytes 1572872 | tf_op jit(solution)/shard_map/ppermute | solution.py:75
  75.6 1.3 %update.1 = (bf16[1024,128]{1,0:T(8,128)(2,1)}, bf16[1152,128]{1,0:T(8,128)(2,1)S(1)}) custom-call(bf16[2,1024,128]{2,1,0:T(8,128)(2,1)S(1)} %get-tuple-element.8.keep_ref, bf16[2,1024,128]{2,1,0:T(8,128)(2,1)S(1)} %collective-permute-done.1.received_ref.second_in_ref, bf16[1024,128]{1,0:T(8,128)(2,1)S(1)} %collective-permute-done.2.third_in_ref, ...), custom_call_target="tpu_custom_call" | custom-call | tf_op jit(solution)/shard_map/update/pallas_call | solution.py:171
  76.9 1.9 %collective-permute-start.4 = (bf16[1152,128]{1,0:T(8,128)(2,1)S(1)}, bf16[1152,128]{1,0:T(8,128)(2,1)S(1)}, u32[]{:S(2)}, u32[]{:S(2)}) collective-permute-start(bf16[1152,128]{1,0:T(8,128)(2,1)S(1)} %get-tuple-element.13.own_ref), channel_id=1, source_target_pairs={{0,16},{16,0},{32,48},{48,32},{64,80},{80,64},{96,112},{112,96},{1... | collective-permute-start | bytes 884744 | tf_op jit(solution)/shard_map/ppermute | solution.py:75
  79.0 3.6 %collective-permute-done.3.far_ref = bf16[8,32,1024]{2,1,0:T(8,128)(2,1)S(1)} collective-permute-done((bf16[8,32,1024]{2,1,0:T(8,128)(2,1)S(1)}, bf16[8,32,1024]{2,1,0:T(8,128)(2,1)S(1)}, u32[]{:S(2)}, u32[]{:S(2)}) %collective-permute-start.3) | collective-permute-done | bytes 524320 | tf_op jit(solution)/shard_map/ppermute | solution.py:75
  82.6 2.0 %project.1 = bf16[16,2,32,128]{3,2,1,0:T(8,128)(2,1)} custom-call(s32[17]{0:T(128)S(1)} %pad_add_fusion.order_ref, bf16[8,32,1024]{2,1,0:T(8,128)(2,1)S(1)} %bitcast.34, bf16[8,32,1024]{2,1,0:T(8,128)(2,1)S(1)} %collective-permute-done.3.far_ref, bf16[1152,128]{1,0:T(8,128)(2,1)S(1)} %get-tuple-element.13.own_ref, ...), custom_call_target="tpu_custom_call" | custom-call | tf_op jit(solution)/shard_map/project/pallas_call | solution.py:206
  84.5 6.9 %all-to-all-start = ((bf16[16,2,32,128]{3,2,1,0:T(8,128)(2,1)}), bf16[16,2,32,128]{3,2,1,0:T(8,128)(2,1)S(1)}, u32[]{:S(2)}, u32[]{:S(2)}) async-start(bf16[16,2,32,128]{3,2,1,0:T(8,128)(2,1)} %project.1), calls=%async_computation | async-start | bytes 524288 | tf_op jit(solution)/shard_map/all_to_all | solution.py:396
  91.8 8.2 %all-to-all-done.parts_ref = bf16[16,2,32,128]{3,2,1,0:T(8,128)(2,1)S(1)} async-done(((bf16[16,2,32,128]{3,2,1,0:T(8,128)(2,1)}), bf16[16,2,32,128]{3,2,1,0:T(8,128)(2,1)S(1)}, u32[]{:S(2)}, u32[]{:S(2)}) %all-to-all-start) | async-done | bytes 262176 | tf_op jit(solution)/shard_map/all_to_all | solution.py:396
  100.0 8.7 %collective-permute-start.5 = (bf16[2,32,128]{2,1,0:T(8,128)(2,1)S(1)}, bf16[2,32,128]{2,1,0:T(8,128)(2,1)S(1)}, u32[]{:S(2)}, u32[]{:S(2)}) collective-permute-start(bf16[2,32,128]{2,1,0:T(8,128)(2,1)S(1)} %unit_sum.1), channel_id=1, source_target_pairs={{10,0},{11,32},{6,64},{13,96},{7,128},{2,160},{4,192},{1,224},{0,2... | collective-permute-start | bytes 49160 | tf_op jit(solution)/shard_map/ppermute | solution.py:397
  108.7 13.8 %all-gather = bf16[3136,128]{1,0:T(8,128)(2,1)S(1)} all-gather(bf16[784,128]{1,0:T(8,128)(2,1)S(1)} %fusion.1), channel_id=2, replica_groups={{0,1,2,3},{4,5,6,7},{8,9,10,11},{12,13,14,15},{16,17,18,19},{20,21,22,2..., dimensions={0}, use_global_device_ids=true | all-gather | bytes 1003520 | tf_op jit(solution)/shard_map/all_gather | solution.py:386
  122.4 1.3 %attend.1.attention_ref = f32[32,256]{1,0:T(8,128)S(1)} custom-call(s32[32,128]{1,0:T(8,128)S(1)} %add_add_fusion.marks_ref, bf16[4,32,256]{2,1,0:T(8,128)(2,1)S(1)} %copy-done.5, bf16[4,784,128]{2,1,0:T(8,128)(2,1)S(1)} %bitcast.32), custom_call_target="tpu_custom_call" | custom-call | tf_op jit(solution)/shard_map/attend/pallas_call | solution.py:336
  123.7 0.6 finish.1
  (45 shorter events, 1.0 us)
Async XLA Ops:
  1.3 1.6 %copy-start = (bf16[1,1024,1024]{2,1,0:T(8,128)(2,1)S(1)}, bf16[1,1024,1024]{2,1,0:T(8,128)(2,1)}, u32[]{:S(2)}) copy-start(bf16[1,1024,1024]{2,1,0:T(8,128)(2,1)} %param.14) | copy-start | bytes 6291460
  2.9 5.6 %copy-start.1 = (bf16[1,1024,1024]{2,1,0:T(8,128)(2,1)S(1)}, bf16[1,1024,1024]{2,1,0:T(8,128)(2,1)}, u32[]{:S(2)}) copy-start(bf16[1,1024,1024]{2,1,0:T(8,128)(2,1)} %param.14) | copy-start | bytes 6291460
  3.9 4.6 %collective-permute-start = (bf16[4,1024,128]{2,1,0:T(8,128)(2,1)S(1)}, bf16[4,1024,128]{2,1,0:T(8,128)(2,1)S(1)}, u32[]{:S(2)}, u32[]{:S(2)}) collective-permute-start(bf16[4,1024,128]{2,1,0:T(8,128)(2,1)S(1)} %take_chunks.1), channel_id=1, source_target_pairs={{0,16},{16,0},{32,48},{48,32},{64,80},{80,64},{96,112},{112,96},{1... | collective-permute-start | bytes 3145736 | tf_op jit(solution)/shard_map/ppermute | solution.py:75
  8.5 8.8 %copy-start.10 = (bf16[4,32,2,32]{3,2,1,0:T(2,128)(2,1)S(1)}, bf16[4,32,2,32]{3,2,1,0:T(2,128)(2,1)}, u32[]{:S(2)}) copy-start(bf16[4,32,2,32]{3,2,1,0:T(2,128)(2,1)} %param.21) | copy-start | bytes 49156
  8.5 9.1 %copy-start.11 = (bf16[32,2,8]{0,2,1:T(8,128)(2,1)S(1)}, bf16[32,2,8]{0,2,1:T(8,128)(2,1)}, u32[]{:S(2)}) copy-start(bf16[32,2,8]{0,2,1:T(8,128)(2,1)} %param.24) | copy-start | bytes 3076
  8.5 9.3 %copy-start.7 = (bf16[4,32,1024]{2,1,0:T(8,128)(2,1)S(1)}, bf16[4,32,1024]{2,1,0:T(8,128)(2,1)}, u32[]{:S(2)}) copy-start(bf16[4,32,1024]{2,1,0:T(8,128)(2,1)} %param.19) | copy-start | bytes 786436
  9.7 65.8 %copy-start.12 = (s32[32]{0:T(128)S(1)}, s32[32]{0:T(128)}, u32[]{:S(2)}) copy-start(s32[32]{0:T(128)} %param.25) | copy-start | bytes 388
  9.7 65.9 %copy-start.2 = (f32[1024,128]{1,0:T(8,128)S(1)}, f32[1024,128]{1,0:T(8,128)}, u32[]{:S(2)}) copy-start(f32[1024,128]{1,0:T(8,128)} %master_ref.1) | copy-start | bytes 1572868
  9.7 65.9 %copy-start.3 = (f32[1024,128]{1,0:T(8,128)S(1)}, f32[1024,128]{1,0:T(8,128)}, u32[]{:S(2)}) copy-start(f32[1024,128]{1,0:T(8,128)} %moment_ref.1) | copy-start | bytes 1572868
  9.7 65.9 %copy-start.4 = (f32[1024,128]{1,0:T(8,128)S(1)}, f32[1024,128]{1,0:T(8,128)}, u32[]{:S(2)}) copy-start(f32[1024,128]{1,0:T(8,128)} %second_ref.1) | copy-start | bytes 1572868
  9.7 19.7 %collective-permute-start.1 = (bf16[2,1024,128]{2,1,0:T(8,128)(2,1)S(1)}, bf16[2,1024,128]{2,1,0:T(8,128)(2,1)S(1)}, u32[]{:S(2)}, u32[]{:S(2)}) collective-permute-start(bf16[2,1024,128]{2,1,0:T(8,128)(2,1)S(1)} %get-tuple-element.9), channel_id=1, source_target_pairs={{0,32},{16,48},{32,0},{48,16},{64,96},{80,112},{96,64},{112,80},{1... | collective-permute-start | bytes 1572872 | tf_op jit(solution)/shard_map/ppermute | solution.py:75
  29.5 46.1 %collective-permute-start.2 = (bf16[1024,128]{1,0:T(8,128)(2,1)S(1)}, bf16[1024,128]{1,0:T(8,128)(2,1)S(1)}, u32[]{:S(2)}, u32[]{:S(2)}) collective-permute-start(bf16[1024,128]{1,0:T(8,128)(2,1)S(1)} %pair_sum.1), channel_id=1, source_target_pairs={{0,64},{16,80},{32,96},{48,112},{64,0},{80,16},{96,32},{112,48},{1... | collective-permute-start | bytes 786440 | tf_op jit(solution)/shard_map/ppermute | solution.py:75
  70.8 11.8 %collective-permute-start.3 = (bf16[8,32,1024]{2,1,0:T(8,128)(2,1)S(1)}, bf16[8,32,1024]{2,1,0:T(8,128)(2,1)S(1)}, u32[]{:S(2)}, u32[]{:S(2)}) collective-permute-start(bf16[8,32,1024]{2,1,0:T(8,128)(2,1)S(1)} %bitcast.33), channel_id=1, source_target_pairs={{0,32},{16,48},{32,0},{48,16},{64,96},{80,112},{96,64},{112,80},{1... | collective-permute-start | bytes 1572872 | tf_op jit(solution)/shard_map/ppermute | solution.py:75
  75.5 15.9 %copy-start.8 = (bf16[32,8,128]{2,1,0:T(8,128)(2,1)S(1)}, bf16[32,8,128]{2,1,0:T(8,128)(2,1)}, u32[]{:S(2)}) copy-start(bf16[32,8,128]{2,1,0:T(8,128)(2,1)} %param.23) | copy-start | bytes 196612
  75.5 15.9 %copy-start.9 = (bf16[32,8,128]{2,1,0:T(8,128)(2,1)S(1)}, bf16[32,8,128]{2,1,0:T(8,128)(2,1)}, u32[]{:S(2)}) copy-start(bf16[32,8,128]{2,1,0:T(8,128)(2,1)} %param.22) | copy-start | bytes 196612
  76.9 5.7 %collective-permute-start.4 = (bf16[1152,128]{1,0:T(8,128)(2,1)S(1)}, bf16[1152,128]{1,0:T(8,128)(2,1)S(1)}, u32[]{:S(2)}, u32[]{:S(2)}) collective-permute-start(bf16[1152,128]{1,0:T(8,128)(2,1)S(1)} %get-tuple-element.13.own_ref), channel_id=1, source_target_pairs={{0,16},{16,0},{32,48},{48,32},{64,80},{80,64},{96,112},{112,96},{1... | collective-permute-start | bytes 884744 | tf_op jit(solution)/shard_map/ppermute | solution.py:75
  78.9 43.5 %copy-start.5 = (bf16[4,32,256]{2,1,0:T(8,128)(2,1)S(1)}, bf16[4,32,256]{2,1,0:T(8,128)(2,1)}, u32[]{:S(2)}) copy-start(bf16[4,32,256]{2,1,0:T(8,128)(2,1)} %queries_ref.1) | copy-start | bytes 196612
  79.0 44.8 %copy-start.6 = (bf16[32,256]{1,0:T(8,128)(2,1)S(1)}, bf16[32,256]{1,0:T(8,128)(2,1)}, u32[]{:S(2)}) copy-start(bf16[32,256]{1,0:T(8,128)(2,1)} %state_ref.1) | copy-start | bytes 49156
  84.5 15.4 %all-to-all-start = ((bf16[16,2,32,128]{3,2,1,0:T(8,128)(2,1)}), bf16[16,2,32,128]{3,2,1,0:T(8,128)(2,1)S(1)}, u32[]{:S(2)}, u32[]{:S(2)}) async-start(bf16[16,2,32,128]{3,2,1,0:T(8,128)(2,1)} %project.1), calls=%async_computation | async-start | bytes 524288 | tf_op jit(solution)/shard_map/all_to_all | solution.py:396
  100.0 23.7 %collective-permute-start.5 = (bf16[2,32,128]{2,1,0:T(8,128)(2,1)S(1)}, bf16[2,32,128]{2,1,0:T(8,128)(2,1)S(1)}, u32[]{:S(2)}, u32[]{:S(2)}) collective-permute-start(bf16[2,32,128]{2,1,0:T(8,128)(2,1)S(1)} %unit_sum.1), channel_id=1, source_target_pairs={{10,0},{11,32},{6,64},{13,96},{7,128},{2,160},{4,192},{1,224},{0,2... | collective-permute-start | bytes 49160 | tf_op jit(solution)/shard_map/ppermute | solution.py:397

commit v2 on v1

--- a/solution.py
+++ b/solution.py
@@ -75,6 +75,11 @@
     return lax.ppermute(value, "dp", [(s, s ^ mask) for s in range(8)])
 
 
+def from_plane(value, ahead):
+    count = 2 * CHIPS
+    return lax.ppermute(value, Z, [((d + 2 * ahead) % count, d) for d in range(count)])
+
+
 def split_kernel(index_ref, grad_ref, out_ref):
     out_ref[0] = grad_ref[...]
 
@@ -130,6 +135,7 @@
         out_specs=pl.BlockSpec((UNITS, BLK), lambda i: (0, 0)),
         out_shape=jax.ShapeDtypeStruct((UNITS, BLK), BF16),
         compiler_params=params(),
+        cost_estimate=pl.CostEstimate(flops=10**11, bytes_accessed=10**9, transcendentals=0),
         name="pair_sum",
     )(keep, received)
 
@@ -182,45 +188,42 @@
     )(keep, second_in, third_in, master, moment, second)
 
 
-def project_kernel(order_ref, near_ref, far_ref, own_ref, other_ref, out_ref, sums):
-    half = CHIPS // 2
+def project_kernel(order_ref, same_ref, up_ref, two_low_ref, two_high_ref, down_ref, own_ref, other_ref, out_ref, sums):
     core = order_ref[CHIPS]
-    for side, rows_ref in enumerate((near_ref, far_ref)):
+    start = 0
+    for rows_ref in (same_ref, up_ref, two_low_ref, two_high_ref, down_ref):
+        count = rows_ref.shape[0]
         for which, codes_ref in enumerate((own_ref, other_ref)):
-            total = jnp.zeros((half * ROWS, BLK), F32)
+            total = jnp.zeros((count * ROWS, BLK), F32)
             for block in range(UNITS // BLK):
-                rows = rows_ref[:, :, block * BLK : (block + 1) * BLK].reshape(half * ROWS, BLK)
+                rows = rows_ref[:, :, block * BLK : (block + 1) * BLK].reshape(count * ROWS, BLK)
                 codes = codes_ref[block * BLK : (block + 1) * BLK]
                 scale = codes_ref[UNITS + 16 * block : UNITS + 16 * (block + 1)][:1].astype(F32)
                 total = total + jnp.dot(rows, codes, preferred_element_type=F32) * scale
-            sums[which, side * half : (side + 1) * half] = total.astype(BF16).reshape(
-                half, ROWS, BLK
-            )
+            sums[which, start : start + count] = total.astype(BF16).reshape(count, ROWS, BLK)
+        start += count
     for place in range(CHIPS):
         row_block = order_ref[place]
         out_ref[place, core] = sums[0, row_block]
         out_ref[place, 1 - core] = sums[1, row_block]
 
 
-def project(order, near, far, own, other):
+def project(order, row_sets, own, other):
+    rows = lambda x: pl.BlockSpec(x.shape, lambda i, order: (0, 0, 0))
+    packed = pl.BlockSpec((PACKED, BLK), lambda i, order: (0, 0))
     return pl.pallas_call(
         project_kernel,
         grid_spec=pltpu.PrefetchScalarGridSpec(
             num_scalar_prefetch=1,
             grid=(1,),
-            in_specs=[
-                pl.BlockSpec((CHIPS // 2, ROWS, UNITS), lambda i, order: (0, 0, 0)),
-                pl.BlockSpec((CHIPS // 2, ROWS, UNITS), lambda i, order: (0, 0, 0)),
-                pl.BlockSpec((PACKED, BLK), lambda i, order: (0, 0)),
-                pl.BlockSpec((PACKED, BLK), lambda i, order: (0, 0)),
-            ],
+            in_specs=[rows(x) for x in row_sets] + [packed, packed],
             out_specs=pl.BlockSpec((CHIPS, 2, ROWS, BLK), lambda i, order: (0, 0, 0, 0)),
             scratch_shapes=[pltpu.VMEM((2, CHIPS, ROWS, BLK), BF16)],
         ),
         out_shape=jax.ShapeDtypeStruct((CHIPS, 2, ROWS, BLK), BF16),
         compiler_params=params(),
         name="project",
-    )(order, near, far, own, other)
+    )(order, *[pltpu.with_memory_space_constraint(x, pltpu.HBM) for x in row_sets], own, other)
 
 
 def unit_sum_kernel(parts_ref, out_ref):
@@ -257,33 +260,63 @@
 
 
 KEYS = ROWS * SLOTS
-FRESH = STEPS * ROWS
-KV_ROWS = 2 * KEYS + 2 * FRESH + 16
+FRESH = 2 * STEPS * ROWS
+SCALES_AT = 2 * KEYS + FRESH
+CACHE_ROWS = SCALES_AT + 16
+
+
+def pack_kernel(place_ref, keys_ref, values_ref, scale_ref, fresh_ref, out_ref):
+    out_ref[:KEYS] = keys_ref[...]
+    out_ref[KEYS : 2 * KEYS] = values_ref[...]
+    width = fresh_ref.shape[1]
+    wide = jnp.concatenate([fresh_ref[...].astype(F32)] * (HD // width), axis=1)
+    lane = lax.broadcasted_iota(jnp.int32, wide.shape, 1)
+    out_ref[2 * KEYS : SCALES_AT] = jnp.where(lane // width == place_ref[0], wide, 0.0).astype(BF16)
+    spread = lax.broadcasted_iota(jnp.int32, (ROWS, KEYS), 1) // SLOTS
+    spread = (spread == lax.broadcasted_iota(jnp.int32, (ROWS, KEYS), 0)).astype(BF16)
+    lines = jnp.dot(scale_ref[...], spread, preferred_element_type=F32)
+    slot = lax.broadcasted_iota(jnp.int32, lines.shape, 0) & (SLOTS - 1)
+    lane = lax.broadcasted_iota(jnp.int32, lines.shape, 1) & (SLOTS - 1)
+    lines = jnp.where(slot == lane, lines, 0.0)
+    rows = [
+        jnp.sum(lines[k * SLOTS : (k + 1) * SLOTS, i * HD : (i + 1) * HD], axis=0, keepdims=True)
+        for k in range(2)
+        for i in range(KEYS // HD)
+    ]
+    out_ref[SCALES_AT:] = jnp.concatenate(
+        rows + [jnp.zeros((16 - len(rows), HD), F32)], axis=0
+    ).astype(BF16)
 
 
 def pack_caches(cache_k, cache_v, cache_scale, fresh_kv, place):
-    width = fresh_kv.shape[3]
-    fresh = fresh_kv.transpose(2, 0, 1, 3).reshape(2 * FRESH, width)
-    lane = lax.broadcasted_iota(jnp.int32, (2 * FRESH, HD), 1)
-    fresh = jnp.where(lane // width == place, jnp.tile(fresh, (1, HD // width)), 0)
-    scale = cache_scale.transpose(1, 0, 2).reshape(2 * KEYS // HD, HD)
-    scale = jnp.pad(scale, ((0, 16 - scale.shape[0]), (0, 0)))
-    return jnp.concatenate(
-        [cache_k.reshape(KEYS, HD), cache_v.reshape(KEYS, HD), fresh, scale], axis=0
+    vmem = pl.BlockSpec(memory_space=pltpu.VMEM)
+    return pl.pallas_call(
+        pack_kernel,
+        in_specs=[pl.BlockSpec(memory_space=pltpu.SMEM)] + [vmem] * 4,
+        out_specs=vmem,
+        out_shape=jax.ShapeDtypeStruct((CACHE_ROWS, HD), BF16),
+        compiler_params=params(),
+        name="pack_caches",
+    )(
+        place[None],
+        cache_k.reshape(KEYS, HD),
+        cache_v.reshape(KEYS, HD),
+        cache_scale.transpose(1, 2, 0).reshape(2 * SLOTS, ROWS),
+        fresh_kv.reshape(FRESH, fresh_kv.shape[3]),
     )
 
 
-def attend_kernel(marks_ref, queries_ref, packed_ref, out_ref):
+def attend_kernel(lengths_ref, queries_ref, packed_ref, out_ref):
     inv = 1.0 / math.sqrt(HD)
     slots = QUADS * KEYS
     keys = packed_ref[:, :KEYS].reshape(slots, HD)
     values = packed_ref[:, KEYS : 2 * KEYS].reshape(slots, HD)
-    fresh = packed_ref[0, 2 * KEYS : 2 * KEYS + 2 * FRESH].astype(F32)
+    fresh = packed_ref[0, 2 * KEYS : SCALES_AT].astype(F32)
     for place in range(1, QUADS):
-        fresh = fresh + packed_ref[place, 2 * KEYS : 2 * KEYS + 2 * FRESH].astype(F32)
-    fresh = fresh.astype(BF16)
-    new_keys, new_values = fresh[:FRESH], fresh[FRESH:]
-    scales = packed_ref[:, 2 * KEYS + 2 * FRESH :].astype(F32)
+        fresh = fresh + packed_ref[place, 2 * KEYS : SCALES_AT].astype(F32)
+    new_keys = fresh.astype(BF16)
+    new_values = pltpu.roll(fresh, FRESH - 1, 0).astype(BF16)
+    scales = packed_ref[:, SCALES_AT:].astype(F32)
     lines = KEYS // HD
     key_scale = jnp.concatenate(
         [scales[p, i : i + 1] for p in range(QUADS) for i in range(lines)], axis=1
@@ -291,19 +324,28 @@
     value_scale = jnp.concatenate(
         [scales[p, lines + i : lines + i + 1] for p in range(QUADS) for i in range(lines)], axis=1
     )
+    row = lax.broadcasted_iota(jnp.int32, (ROWS, ROWS), 0)
+    column = lax.broadcasted_iota(jnp.int32, (ROWS, ROWS), 1)
+    length = jnp.where(row == column, lengths_ref[...].astype(F32), 0.0)
+    length = jnp.sum(length, axis=1, keepdims=True).astype(jnp.int32)
     lane = lax.broadcasted_iota(jnp.int32, (ROWS, slots), 1)
     row = lax.broadcasted_iota(jnp.int32, (ROWS, slots), 0)
     slot = (lane // KEYS) * SLOTS + (lane & (SLOTS - 1))
     live = ((lane // SLOTS) & (ROWS - 1)) == row
-    live = live & (slot < marks_ref[:, 0:1])
-    new_lane = lax.broadcasted_iota(jnp.int32, (ROWS, FRESH), 1)
-    new_row = lax.broadcasted_iota(jnp.int32, (ROWS, FRESH), 0)
-    mine = (new_lane & (ROWS - 1)) == new_row
+    live = live & (slot < length)
+    ahead = slot - length
+    window = CACHE - SINK
+    lane = lax.broadcasted_iota(jnp.int32, (ROWS, FRESH), 1)
+    row = lax.broadcasted_iota(jnp.int32, (ROWS, FRESH), 0)
+    mine = (((lane // 2) & (ROWS - 1)) == row) & ((lane & 1) == 0)
     old_sum = [jnp.zeros((ROWS, slots), F32) for _ in range(2)]
     new_sum = [jnp.zeros((ROWS, FRESH), F32) for _ in range(2)]
     for step in range(STEPS):
-        live = live & (slot != marks_ref[:, step + 1 : step + 2])
-        seen = mine & (new_lane // ROWS <= step)
+        evicted = ahead == step
+        for turn in range(1, (4 * CACHE + STEPS) // window + 1):
+            evicted = evicted | (ahead == step - turn * window)
+        live = live & jnp.logical_not(evicted & (slot >= SINK))
+        seen = mine & (lane // (2 * ROWS) <= step)
         for head in range(2):
             query = queries_ref[step, :, head * HD : (head + 1) * HD]
             across = (((1,), (1,)), ((), ()))
@@ -328,17 +370,12 @@
 
 
 def attend(lengths, queries, packed):
-    steps = jnp.arange(STEPS, dtype=jnp.int32)
-    evicted = SINK + (lengths[:, None] + steps[None, :] - SINK) % (CACHE - SINK)
-    marks = jnp.concatenate(
-        [lengths[:, None], evicted, jnp.zeros((ROWS, HD - 1 - STEPS), jnp.int32)], axis=1
-    )
     return pl.pallas_call(
         attend_kernel,
         out_shape=jax.ShapeDtypeStruct((ROWS, 2 * HD), F32),
         compiler_params=params(),
         name="attend",
-    )(marks, queries, packed)
+    )(lengths[None], queries, packed)
 
 
 def shards(
@@ -363,36 +400,40 @@
 
     owners = low ^ jnp.array([0, 2, 1, 3], jnp.int32)
     outgoing = take_chunks(2 * owners + 1 - core, grad)
-    units = jnp.sum(hidden.astype(F32), axis=0).astype(BF16)
     received = flip(outgoing, 1)
     keep, send = core_sum(2 * owners + core, grad, received)
     second_in = flip(send, 2)
 
-    units, send = lax.optimization_barrier((units, send))
-    parity_groups = [
-        [g * 8 + (2 * h + l) * 2 + b for g in range(4) for h in range(2)]
-        for l in range(2)
-        for b in range(2)
-    ]
-    near = lax.all_gather(units, Z, axis=0, axis_index_groups=parity_groups)
+    hidden, _ = lax.optimization_barrier((hidden, send))
+    units = jnp.sum(hidden.astype(F32), axis=0).astype(BF16)
+    same = jnp.broadcast_to(units, (4,) + units.shape)
+    same = lax.all_to_all(same, "grp", 0, 0)
+
+    caches = pack_caches(cache_k, cache_v, cache_scale, fresh_kv, tp % QUADS)
+    caches = jnp.broadcast_to(caches, (QUADS,) + caches.shape)
+    caches, _ = lax.optimization_barrier((caches, send))
+    quads = [[QUADS * x + y for y in range(QUADS)] for x in range(QUADS)]
+    packed = lax.all_to_all(caches, "tp", 0, 0, axis_index_groups=quads)
 
     third = pair_sum(keep, second_in)
     third_in = flip(third, 4)
-    far = flip(near, 2)
-
-    caches = pack_caches(cache_k, cache_v, cache_scale, fresh_kv, tp % QUADS)
-    caches, _ = lax.optimization_barrier((caches, third))
-    quads = [[QUADS * x + y for y in range(QUADS)] for x in range(QUADS)]
-    packed = lax.all_gather(caches, "tp", axis=0, axis_index_groups=quads)
+    same, _ = lax.optimization_barrier((same, third))
+    up = from_plane(same, 1)
+    down = from_plane(same, -1)
+    two_low = from_plane(same[:2], 2)
+    two_high = from_plane(same[2:], -2)
     attention = attend(lengths, queries, packed)
 
+    third_in, up, down, two_low, two_high = lax.optimization_barrier(
+        (third_in, up, down, two_low, two_high)
+    )
     codes, own = update(keep, second_in, third_in, master, moment, second)
     other = flip(own, 1)
 
     row_at = lax.dynamic_index_in_dim(jnp.array(ROW_AT), plane, 0, keepdims=False)
-    order = ((row_at ^ low) & 1) * (CHIPS // 2) + row_at // 2
+    order = ((row_at - low) & 3) * 4 + row_at // 4
     order = jnp.concatenate([order, core[None]]).astype(jnp.int32)
-    parts = project(order, near, far, own, other)
+    parts = project(order, (same, up, two_low, two_high, down), own, other)
     parts = lax.all_to_all(parts, "tp", 0, 0)
     mixed = lax.ppermute(unit_sum(parts), ALL, home_pairs())
     return (codes, finish(state, attention, mixed))

time: 125 us -> 114 us (0.912)
  the two profiles are of different devices: /device:TPU:32 before, /device:TPU:116 now
where the time goes in v2:
time: 114 us
  starting transfers between devices  54.6 us (48%)
  waiting for transfers between devices  41.9 us (37%)
  Pallas kernels  9.07 us (8%)
  local copies, waits for them, and re-layouts  5.74 us (5%)
  other arithmetic  1.49 us (1%)
    ppermute x4, starting transfers between devices, from_plane(): lax.ppermute(value, Z, [((d + 2 * ahead) % count, d) for d in range(count)])  17 us
    all_to_all x1, waiting for transfers between devices, shards(): same = lax.all_to_all(same, 'grp', 0, 0)  15.2 us
    all_to_all x1, starting transfers between devices, shards(): same = lax.all_to_all(same, 'grp', 0, 0)  13.3 us
    ppermute x4, starting transfers between devices, flip(): return lax.ppermute(value, 'dp', [(s, s ^ mask) for s in range(8)])  9.34 us
    ppermute x4, waiting for transfers between devices, from_plane(): lax.ppermute(value, Z, [((d + 2 * ahead) % count, d) for d in range(count)])  8.44 us
    all_to_all x1, starting transfers between devices, shards(): parts = lax.all_to_all(parts, 'tp', 0, 0)  7.36 us
    all_to_all x1, waiting for transfers between devices, shards(): packed = lax.all_to_all(caches, 'tp', 0, 0, axis_index_groups=quads)  6.46 us
    all_to_all x1, starting transfers between devices, shards(): packed = lax.all_to_all(caches, 'tp', 0, 0, axis_index_groups=quads)  5.48 us
  transfers between devices with their start and end apart: 12, of which 8 were waited for; matrix products, arithmetic and copies ran while one was open for 3% of the time, Pallas kernels for 1%

profile of v2, /device:TPU:116, one launch (start us, length us, event | category | flops | bytes accessed | tf_op | source)
XLA Modules:
  0.0 113.7 jit_solution(7582213346171894204)
XLA Ops:
  1.3 1.6 %copy-done = bf16[1,1024,1024]{2,1,0:T(8,128)(2,1)S(1)} copy-done((bf16[1,1024,1024]{2,1,0:T(8,128)(2,1)S(1)}, bf16[1,1024,1024]{2,1,0:T(8,128)(2,1)}, u32[]{:S(2)}) %copy-start) | copy-done | bytes 2097176
  2.9 1.0 take_chunks.1
  3.9 1.9 %collective-permute-start = (bf16[4,1024,128]{2,1,0:T(8,128)(2,1)S(1)}, bf16[4,1024,128]{2,1,0:T(8,128)(2,1)S(1)}, u32[]{:S(2)}, u32[]{:S(2)}) collective-permute-start(bf16[4,1024,128]{2,1,0:T(8,128)(2,1)S(1)} %take_chunks.1), channel_id=1, source_target_pairs={{0,16},{16,0},{32,48},{48,32},{64,80},{80,64},{96,112},{112,96},{1... | collective-permute-start | bytes 3145736 | tf_op jit(solution)/shard_map/ppermute | solution.py:75
  5.9 2.6 %collective-permute-done.near_in_ref.far_in_ref = bf16[4,1024,128]{2,1,0:T(8,128)(2,1)S(1)} collective-permute-done((bf16[4,1024,128]{2,1,0:T(8,128)(2,1)S(1)}, bf16[4,1024,128]{2,1,0:T(8,128)(2,1)S(1)}, u32[]{:S(2)}, u32[]{:S(2)}) %collective-permute-start) | collective-permute-done | bytes 1048608 | tf_op jit(solution)/shard_map/ppermute | solution.py:75
  8.5 1.1 %core_sum.1 = (bf16[2,1024,128]{2,1,0:T(8,128)(2,1)S(1)}, bf16[2,1024,128]{2,1,0:T(8,128)(2,1)S(1)}) custom-call(s32[4]{0:T(128)S(1)} %get-tuple-element.29.index_ref, bf16[1024,1024]{1,0:T(8,128)(2,1)S(1)} %bitcast.28, bf16[1024,1024]{1,0:T(8,128)(2,1)S(1)} %bitcast.29, bf16[4,1024,128]{2,1,0:T(8,128)(2,1)S(1)} %collective-permute-done.near_in_ref.far_in_ref, ...), custom_call_target="tpu_custom_call" | custom-call | tf_op jit(solution)/shard_map/core_sum/pallas_call | solution.py:111
  9.6 2.0 %collective-permute-start.1 = (bf16[2,1024,128]{2,1,0:T(8,128)(2,1)S(1)}, bf16[2,1024,128]{2,1,0:T(8,128)(2,1)S(1)}, u32[]{:S(2)}, u32[]{:S(2)}) collective-permute-start(bf16[2,1024,128]{2,1,0:T(8,128)(2,1)S(1)} %get-tuple-element.15), channel_id=1, source_target_pairs={{0,32},{16,48},{32,0},{48,16},{64,96},{80,112},{96,64},{112,80},{1... | collective-permute-start | bytes 1572872 | tf_op jit(solution)/shard_map/ppermute | solution.py:75
  12.5 13.3 %all-to-all-start = ((bf16[4,32,1024]{2,1,0:T(8,128)(2,1)}), bf16[4,32,1024]{2,1,0:T(8,128)(2,1)}, u32[]{:S(2)}, u32[]{:S(2)}) async-start(bf16[4,32,1024]{2,1,0:T(8,128)(2,1)} %broadcast_in_dim.15), calls=%async_computation | async-start | bytes 524288 | tf_op jit(solution)/shard_map/all_to_all | solution.py:410
  25.8 3.5 %collective-permute-start.2 = (bf16[1024,128]{1,0:T(8,128)(2,1)S(1)}, bf16[1024,128]{1,0:T(8,128)(2,1)S(1)}, u32[]{:S(2)}, u32[]{:S(2)}) collective-permute-start(bf16[1024,128]{1,0:T(8,128)(2,1)S(1)} %pair_sum.1), channel_id=1, source_target_pairs={{0,64},{16,80},{32,96},{48,112},{64,0},{80,16},{96,32},{112,48},{1... | collective-permute-start | bytes 786440 | tf_op jit(solution)/shard_map/ppermute | solution.py:75
  29.3 15.2 %all-to-all-done.same_ref = bf16[4,32,1024]{2,1,0:T(8,128)(2,1)} async-done(((bf16[4,32,1024]{2,1,0:T(8,128)(2,1)}), bf16[4,32,1024]{2,1,0:T(8,128)(2,1)}, u32[]{:S(2)}, u32[]{:S(2)}) %all-to-all-start) | async-done | bytes 262176 | tf_op jit(solution)/shard_map/all_to_all | solution.py:410
  44.6 1.9 %collective-permute-start.4 = (bf16[4,32,1024]{2,1,0:T(8,128)(2,1)}, bf16[4,32,1024]{2,1,0:T(8,128)(2,1)S(1)}, u32[]{:S(2)}, u32[]{:S(2)}) collective-permute-start(bf16[4,32,1024]{2,1,0:T(8,128)(2,1)} %all-to-all-done.same_ref), channel_id=1, source_target_pairs={{480,0},{496,16},{0,32},{16,48},{32,64},{48,80},{64,96},{80,112},{... | collective-permute-start | bytes 786440 | tf_op jit(solution)/shard_map/ppermute | solution.py:80
  46.5 3.9 %collective-permute-start.3 = (bf16[4,32,1024]{2,1,0:T(8,128)(2,1)}, bf16[4,32,1024]{2,1,0:T(8,128)(2,1)}, u32[]{:S(2)}, u32[]{:S(2)}) collective-permute-start(bf16[4,32,1024]{2,1,0:T(8,128)(2,1)} %all-to-all-done.same_ref), channel_id=1, source_target_pairs={{32,0},{48,16},{64,32},{80,48},{96,64},{112,80},{128,96},{144,112}... | collective-permute-start | bytes 786440 | tf_op jit(solution)/shard_map/ppermute | solution.py:80
  51.4 9.1 %collective-permute-start.6 = (bf16[2,32,1024]{2,1,0:T(8,128)(2,1)S(1)}, bf16[2,32,1024]{2,1,0:T(8,128)(2,1)S(1)}, u32[]{:S(2)}, u32[]{:S(2)}) collective-permute-start(bf16[2,32,1024]{2,1,0:T(8,128)(2,1)S(1)} %get-tuple-element.26), channel_id=1, source_target_pairs={{448,0},{464,16},{480,32},{496,48},{0,64},{16,80},{32,96},{48,112}... | collective-permute-start | bytes 393224 | tf_op jit(solution)/shard_map/ppermute | solution.py:80
  60.6 2.1 %collective-permute-start.5 = (bf16[2,32,1024]{2,1,0:T(8,128)(2,1)S(1)}, bf16[2,32,1024]{2,1,0:T(8,128)(2,1)S(1)}, u32[]{:S(2)}, u32[]{:S(2)}) collective-permute-start(bf16[2,32,1024]{2,1,0:T(8,128)(2,1)S(1)} %get-tuple-element.27), channel_id=1, source_target_pairs={{64,0},{80,16},{96,32},{112,48},{128,64},{144,80},{160,96},{176,11... | collective-permute-start | bytes 393224 | tf_op jit(solution)/shard_map/ppermute | solution.py:80
  63.1 8.1 %collective-permute-done.5.two_low_ref = bf16[2,32,1024]{2,1,0:T(8,128)(2,1)S(1)} collective-permute-done((bf16[2,32,1024]{2,1,0:T(8,128)(2,1)S(1)}, bf16[2,32,1024]{2,1,0:T(8,128)(2,1)S(1)}, u32[]{:S(2)}, u32[]{:S(2)}) %collective-permute-start.5) | collective-permute-done | bytes 131104 | tf_op jit(solution)/shard_map/ppermute | solution.py:80
  72.5 1.3 %update.1 = (bf16[1024,128]{1,0:T(8,128)(2,1)}, bf16[1152,128]{1,0:T(8,128)(2,1)S(1)}) custom-call(bf16[2,1024,128]{2,1,0:T(8,128)(2,1)S(1)} %get-tuple-element.14.keep_ref, bf16[2,1024,128]{2,1,0:T(8,128)(2,1)S(1)} %collective-permute-done.1.received_ref.second_in_ref, bf16[1024,128]{1,0:T(8,128)(2,1)S(1)} %collective-permute-done.2.third_in_ref, ...), custom_call_target="tpu_custom_call" | custom-call | tf_op jit(solution)/shard_map/update/pallas_call | solution.py:177
  73.8 1.9 %collective-permute-start.7 = (bf16[1152,128]{1,0:T(8,128)(2,1)S(1)}, bf16[1152,128]{1,0:T(8,128)(2,1)S(1)}, u32[]{:S(2)}, u32[]{:S(2)}) collective-permute-start(bf16[1152,128]{1,0:T(8,128)(2,1)S(1)} %get-tuple-element.25.own_ref), channel_id=1, source_target_pairs={{0,16},{16,0},{32,48},{48,32},{64,80},{80,64},{96,112},{112,96},{1... | collective-permute-start | bytes 884744 | tf_op jit(solution)/shard_map/ppermute | solution.py:75
  77.3 3.3 %project.1 = bf16[16,2,32,128]{3,2,1,0:T(8,128)(2,1)} custom-call(s32[17]{0:T(128)S(1)} %pad_add_fusion.order_ref, bf16[4,32,1024]{2,1,0:T(8,128)(2,1)} %all-to-all-done.same_ref, bf16[4,32,1024]{2,1,0:T(8,128)(2,1)} %collective-permute-done.3.up_ref, bf16[2,32,1024]{2,1,0:T(8,128)(2,1)} %copy-done.15, bf16[2,32,1024]{2,1,0:T(8,128)(2,1)} %copy-done.14, ...), custom_call_target="tpu_custom_call" | custom-call | tf_op jit(solution)/shard_map/project/pallas_call | solution.py:214
  80.6 7.4 %all-to-all-start.2 = ((bf16[16,2,32,128]{3,2,1,0:T(8,128)(2,1)}), bf16[16,2,32,128]{3,2,1,0:T(8,128)(2,1)S(1)}, u32[]{:S(2)}, u32[]{:S(2)}) async-start(bf16[16,2,32,128]{3,2,1,0:T(8,128)(2,1)} %project.1), calls=%async_computation.2 | async-start | bytes 524288 | tf_op jit(solution)/shard_map/all_to_all | solution.py:437
  89.2 4.0 %all-to-all-done.2.parts_ref = bf16[16,2,32,128]{3,2,1,0:T(8,128)(2,1)S(1)} async-done(((bf16[16,2,32,128]{3,2,1,0:T(8,128)(2,1)}), bf16[16,2,32,128]{3,2,1,0:T(8,128)(2,1)S(1)}, u32[]{:S(2)}, u32[]{:S(2)}) %all-to-all-start.2) | async-done | bytes 262176 | tf_op jit(solution)/shard_map/all_to_all | solution.py:437
  93.2 5.5 %all-to-all-start.1 = ((bf16[4,784,128]{2,1,0:T(8,128)(2,1)}), bf16[4,784,128]{2,1,0:T(8,128)(2,1)S(1)}, u32[]{:S(2)}, u32[]{:S(2)}) async-start(bf16[4,784,128]{2,1,0:T(8,128)(2,1)} %broadcast_in_dim.18), calls=%async_computation.1 | async-start | bytes 1605632 | tf_op jit(solution)/shard_map/all_to_all | solution.py:416
  98.7 2.1 %collective-permute-start.8 = (bf16[2,32,128]{2,1,0:T(8,128)(2,1)S(1)}, bf16[2,32,128]{2,1,0:T(8,128)(2,1)S(1)}, u32[]{:S(2)}, u32[]{:S(2)}) collective-permute-start(bf16[2,32,128]{2,1,0:T(8,128)(2,1)S(1)} %unit_sum.1), channel_id=1, source_target_pairs={{10,0},{11,32},{6,64},{13,96},{7,128},{2,160},{4,192},{1,224},{0,2... | collective-permute-start | bytes 49160 | tf_op jit(solution)/shard_map/ppermute | solution.py:438
  100.8 6.5 %all-to-all-done.1.packed_ref = bf16[4,784,128]{2,1,0:T(8,128)(2,1)S(1)} async-done(((bf16[4,784,128]{2,1,0:T(8,128)(2,1)}), bf16[4,784,128]{2,1,0:T(8,128)(2,1)S(1)}, u32[]{:S(2)}, u32[]{:S(2)}) %all-to-all-start.1) | async-done | bytes 802848 | tf_op jit(solution)/shard_map/all_to_all | solution.py:416
  107.3 1.4 %attend.1.attention_ref = f32[32,256]{1,0:T(8,128)S(1)} custom-call(s32[1,32]{1,0:T(1,128)S(1)} %bitcast.34, bf16[4,32,256]{2,1,0:T(8,128)(2,1)S(1)} %copy-done.8, bf16[4,784,128]{2,1,0:T(8,128)(2,1)S(1)} %all-to-all-done.1.packed_ref), custom_call_target="tpu_custom_call" | custom-call | tf_op jit(solution)/shard_map/attend/pallas_call | solution.py:373
  108.7 4.3 %collective-permute-done.8.mixed_ref = bf16[2,32,128]{2,1,0:T(8,128)(2,1)S(1)} collective-permute-done((bf16[2,32,128]{2,1,0:T(8,128)(2,1)S(1)}, bf16[2,32,128]{2,1,0:T(8,128)(2,1)S(1)}, u32[]{:S(2)}, u32[]{:S(2)}) %collective-permute-start.8) | collective-permute-done | bytes 16416 | tf_op jit(solution)/shard_map/ppermute | solution.py:438
  (48 shorter events, 7.6 us)
Async XLA Ops:
  2.9 5.6 %copy-start.1 = (bf16[1,1024,1024]{2,1,0:T(8,128)(2,1)S(1)}, bf16[1,1024,1024]{2,1,0:T(8,128)(2,1)}, u32[]{:S(2)}) copy-start(bf16[1,1024,1024]{2,1,0:T(8,128)(2,1)} %param.14) | copy-start | bytes 6291460
  3.9 4.6 %collective-permute-start = (bf16[4,1024,128]{2,1,0:T(8,128)(2,1)S(1)}, bf16[4,1024,128]{2,1,0:T(8,128)(2,1)S(1)}, u32[]{:S(2)}, u32[]{:S(2)}) collective-permute-start(bf16[4,1024,128]{2,1,0:T(8,128)(2,1)S(1)} %take_chunks.1), channel_id=1, source_target_pairs={{0,16},{16,0},{32,48},{48,32},{64,80},{80,64},{96,112},{112,96},{1... | collective-permute-start | bytes 3145736 | tf_op jit(solution)/shard_map/ppermute | solution.py:75
  9.6 16.1 %collective-permute-start.1 = (bf16[2,1024,128]{2,1,0:T(8,128)(2,1)S(1)}, bf16[2,1024,128]{2,1,0:T(8,128)(2,1)S(1)}, u32[]{:S(2)}, u32[]{:S(2)}) collective-permute-start(bf16[2,1024,128]{2,1,0:T(8,128)(2,1)S(1)} %get-tuple-element.15), channel_id=1, source_target_pairs={{0,32},{16,48},{32,0},{48,16},{64,96},{80,112},{96,64},{112,80},{1... | collective-permute-start | bytes 1572872 | tf_op jit(solution)/shard_map/ppermute | solution.py:75
  12.5 32.1 %all-to-all-start = ((bf16[4,32,1024]{2,1,0:T(8,128)(2,1)}), bf16[4,32,1024]{2,1,0:T(8,128)(2,1)}, u32[]{:S(2)}, u32[]{:S(2)}) async-start(bf16[4,32,1024]{2,1,0:T(8,128)(2,1)} %broadcast_in_dim.15), calls=%async_computation | async-start | bytes 524288 | tf_op jit(solution)/shard_map/all_to_all | solution.py:410
  25.7 46.7 %copy-start.2 = (f32[1024,128]{1,0:T(8,128)S(1)}, f32[1024,128]{1,0:T(8,128)}, u32[]{:S(2)}) copy-start(f32[1024,128]{1,0:T(8,128)} %master_ref.1) | copy-start | bytes 1572868
  25.7 46.7 %copy-start.3 = (f32[1024,128]{1,0:T(8,128)S(1)}, f32[1024,128]{1,0:T(8,128)}, u32[]{:S(2)}) copy-start(f32[1024,128]{1,0:T(8,128)} %moment_ref.1) | copy-start | bytes 1572868
  25.8 46.7 %copy-start.4 = (f32[1024,128]{1,0:T(8,128)S(1)}, f32[1024,128]{1,0:T(8,128)}, u32[]{:S(2)}) copy-start(f32[1024,128]{1,0:T(8,128)} %second_ref.1) | copy-start | bytes 1572868
  25.8 36.8 %collective-permute-start.2 = (bf16[1024,128]{1,0:T(8,128)(2,1)S(1)}, bf16[1024,128]{1,0:T(8,128)(2,1)S(1)}, u32[]{:S(2)}, u32[]{:S(2)}) collective-permute-start(bf16[1024,128]{1,0:T(8,128)(2,1)S(1)} %pair_sum.1), channel_id=1, source_target_pairs={{0,64},{16,80},{32,96},{48,112},{64,0},{80,16},{96,32},{112,48},{1... | collective-permute-start | bytes 786440 | tf_op jit(solution)/shard_map/ppermute | solution.py:75
  44.6 26.6 %collective-permute-start.4 = (bf16[4,32,1024]{2,1,0:T(8,128)(2,1)}, bf16[4,32,1024]{2,1,0:T(8,128)(2,1)S(1)}, u32[]{:S(2)}, u32[]{:S(2)}) collective-permute-start(bf16[4,32,1024]{2,1,0:T(8,128)(2,1)} %all-to-all-done.same_ref), channel_id=1, source_target_pairs={{480,0},{496,16},{0,32},{16,48},{32,64},{48,80},{64,96},{80,112},{... | collective-permute-start | bytes 786440 | tf_op jit(solution)/shard_map/ppermute | solution.py:80
  46.5 26.0 %collective-permute-start.3 = (bf16[4,32,1024]{2,1,0:T(8,128)(2,1)}, bf16[4,32,1024]{2,1,0:T(8,128)(2,1)}, u32[]{:S(2)}, u32[]{:S(2)}) collective-permute-start(bf16[4,32,1024]{2,1,0:T(8,128)(2,1)} %all-to-all-done.same_ref), channel_id=1, source_target_pairs={{32,0},{48,16},{64,32},{80,48},{96,64},{112,80},{128,96},{144,112}... | collective-permute-start | bytes 786440 | tf_op jit(solution)/shard_map/ppermute | solution.py:80
  51.4 11.7 %collective-permute-start.6 = (bf16[2,32,1024]{2,1,0:T(8,128)(2,1)S(1)}, bf16[2,32,1024]{2,1,0:T(8,128)(2,1)S(1)}, u32[]{:S(2)}, u32[]{:S(2)}) collective-permute-start(bf16[2,32,1024]{2,1,0:T(8,128)(2,1)S(1)} %get-tuple-element.26), channel_id=1, source_target_pairs={{448,0},{464,16},{480,32},{496,48},{0,64},{16,80},{32,96},{48,112}... | collective-permute-start | bytes 393224 | tf_op jit(solution)/shard_map/ppermute | solution.py:80
  60.5 27.4 %copy-start.5 = (bf16[32,8,128]{2,1,0:T(8,128)(2,1)S(1)}, bf16[32,8,128]{2,1,0:T(8,128)(2,1)}, u32[]{:S(2)}) copy-start(bf16[32,8,128]{2,1,0:T(8,128)(2,1)} %param.22) | copy-start | bytes 196612
  60.6 27.4 %copy-start.6 = (bf16[32,8,128]{2,1,0:T(8,128)(2,1)S(1)}, bf16[32,8,128]{2,1,0:T(8,128)(2,1)}, u32[]{:S(2)}) copy-start(bf16[32,8,128]{2,1,0:T(8,128)(2,1)} %param.23) | copy-start | bytes 196612
  60.6 27.4 %copy-start.7 = (bf16[4,32,2,32]{3,2,1,0:T(2,128)(2,1)S(1)}, bf16[4,32,2,32]{3,2,1,0:T(2,128)(2,1)}, u32[]{:S(2)}) copy-start(bf16[4,32,2,32]{3,2,1,0:T(2,128)(2,1)} %param.21) | copy-start | bytes 49156
  60.6 27.4 %copy-start.10 = (bf16[32,2,8]{0,2,1:T(8,128)(2,1)S(1)}, bf16[32,2,8]{0,2,1:T(8,128)(2,1)}, u32[]{:S(2)}) copy-start(bf16[32,2,8]{0,2,1:T(8,128)(2,1)} %param.24) | copy-start | bytes 3076
  60.6 10.5 %collective-permute-start.5 = (bf16[2,32,1024]{2,1,0:T(8,128)(2,1)S(1)}, bf16[2,32,1024]{2,1,0:T(8,128)(2,1)S(1)}, u32[]{:S(2)}, u32[]{:S(2)}) collective-permute-start(bf16[2,32,1024]{2,1,0:T(8,128)(2,1)S(1)} %get-tuple-element.27), channel_id=1, source_target_pairs={{64,0},{80,16},{96,32},{112,48},{128,64},{144,80},{160,96},{176,11... | collective-permute-start | bytes 393224 | tf_op jit(solution)/shard_map/ppermute | solution.py:80
  63.0 14.2 %copy-start.14 = (bf16[2,32,1024]{2,1,0:T(8,128)(2,1)}, bf16[2,32,1024]{2,1,0:T(8,128)(2,1)S(1)}, u32[]{:S(2)}) copy-start(bf16[2,32,1024]{2,1,0:T(8,128)(2,1)S(1)} %collective-permute-done.6.two_high_ref) | copy-start | bytes 393220
  73.8 3.5 %collective-permute-start.7 = (bf16[1152,128]{1,0:T(8,128)(2,1)S(1)}, bf16[1152,128]{1,0:T(8,128)(2,1)S(1)}, u32[]{:S(2)}, u32[]{:S(2)}) collective-permute-start(bf16[1152,128]{1,0:T(8,128)(2,1)S(1)} %get-tuple-element.25.own_ref), channel_id=1, source_target_pairs={{0,16},{16,0},{32,48},{48,32},{64,80},{80,64},{96,112},{112,96},{1... | collective-permute-start | bytes 884744 | tf_op jit(solution)/shard_map/ppermute | solution.py:75
  80.6 26.7 %copy-start.8 = (bf16[4,32,256]{2,1,0:T(8,128)(2,1)S(1)}, bf16[4,32,256]{2,1,0:T(8,128)(2,1)}, u32[]{:S(2)}) copy-start(bf16[4,32,256]{2,1,0:T(8,128)(2,1)} %queries_ref.1) | copy-start | bytes 196612
  80.6 26.7 %copy-start.11 = (s32[32]{0:T(128)S(1)}, s32[32]{0:T(128)}, u32[]{:S(2)}) copy-start(s32[32]{0:T(128)} %param.25) | copy-start | bytes 388
  80.6 12.6 %all-to-all-start.2 = ((bf16[16,2,32,128]{3,2,1,0:T(8,128)(2,1)}), bf16[16,2,32,128]{3,2,1,0:T(8,128)(2,1)S(1)}, u32[]{:S(2)}, u32[]{:S(2)}) async-start(bf16[16,2,32,128]{3,2,1,0:T(8,128)(2,1)} %project.1), calls=%async_computation.2 | async-start | bytes 524288 | tf_op jit(solution)/shard_map/all_to_all | solution.py:437
  88.0 25.1 %copy-start.9 = (bf16[32,256]{1,0:T(8,128)(2,1)S(1)}, bf16[32,256]{1,0:T(8,128)(2,1)}, u32[]{:S(2)}) copy-start(bf16[32,256]{1,0:T(8,128)(2,1)} %state_ref.1) | copy-start | bytes 49156
  93.2 14.1 %all-to-all-start.1 = ((bf16[4,784,128]{2,1,0:T(8,128)(2,1)}), bf16[4,784,128]{2,1,0:T(8,128)(2,1)S(1)}, u32[]{:S(2)}, u32[]{:S(2)}) async-start(bf16[4,784,128]{2,1,0:T(8,128)(2,1)} %broadcast_in_dim.18), calls=%async_computation.1 | async-start | bytes 1605632 | tf_op jit(solution)/shard_map/all_to_all | solution.py:416
  98.7 14.4 %collective-permute-start.8 = (bf16[2,32,128]{2,1,0:T(8,128)(2,1)S(1)}, bf16[2,32,128]{2,1,0:T(8,128)(2,1)S(1)}, u32[]{:S(2)}, u32[]{:S(2)}) collective-permute-start(bf16[2,32,128]{2,1,0:T(8,128)(2,1)S(1)} %unit_sum.1), channel_id=1, source_target_pairs={{10,0},{11,32},{6,64},{13,96},{7,128},{2,160},{4,192},{1,224},{0,2... | collective-permute-start | bytes 49160 | tf_op jit(solution)/shard_map/ppermute | solution.py:438
  (4 other events, 6.2 us)

commit v3 on v2

--- a/solution.py
+++ b/solution.py
@@ -99,27 +99,39 @@
     )(index, grad)
 
 
-def core_sum_kernel(index_ref, near_ref, far_ref, near_in_ref, far_in_ref, keep_ref, send_ref):
+def core_sum_kernel(
+    index_ref, near_ref, far_ref, near_in_ref, far_in_ref, hidden_ref, keep_ref, send_ref, units_ref
+):
     keep_ref[0] = (near_ref[...].astype(F32) + near_in_ref[0].astype(F32)).astype(BF16)
     send_ref[0] = (far_ref[...].astype(F32) + far_in_ref[0].astype(F32)).astype(BF16)
 
-
-def core_sum(index, grad, received):
+    @pl.when(pl.program_id(0) == 0)
+    def _():
+        total = hidden_ref[0].astype(F32)
+        for step in range(1, STEPS):
+            total = total + hidden_ref[step].astype(F32)
+        total = total.astype(BF16)
+        for run in range(4):
+            units_ref[run] = total
+
+
+def core_sum(index, grad, received, hidden):
     whole = lambda shift: pl.BlockSpec((UNITS, BLK), lambda j, index: (0, index[j + shift]))
     part = lambda shift: pl.BlockSpec((1, UNITS, BLK), lambda j, index: (j + shift, 0, 0))
+    every = pl.BlockSpec(hidden.shape, lambda j, index: (0, 0, 0))
     shape = jax.ShapeDtypeStruct((2, UNITS, BLK), BF16)
     return pl.pallas_call(
         core_sum_kernel,
         grid_spec=pltpu.PrefetchScalarGridSpec(
             num_scalar_prefetch=1,
             grid=(2,),
-            in_specs=[whole(0), whole(2), part(0), part(2)],
-            out_specs=[part(0), part(0)],
+            in_specs=[whole(0), whole(2), part(0), part(2), every],
+            out_specs=[part(0), part(0), every],
         ),
-        out_shape=[shape, shape],
+        out_shape=[shape, shape, jax.ShapeDtypeStruct(hidden.shape, BF16)],
         compiler_params=params(),
         name="core_sum",
-    )(index, grad, grad, received, received)
+    )(index, grad, grad, received, received, hidden)
 
 
 def pair_sum_kernel(keep_ref, received_ref, out_ref):
@@ -184,6 +196,7 @@
             jax.ShapeDtypeStruct((PACKED, BLK), BF16),
         ],
         compiler_params=params(),
+        cost_estimate=pl.CostEstimate(flops=10**11, bytes_accessed=10**9, transcendentals=0),
         name="update",
     )(keep, second_in, third_in, master, moment, second)
 
@@ -223,7 +236,7 @@
         out_shape=jax.ShapeDtypeStruct((CHIPS, 2, ROWS, BLK), BF16),
         compiler_params=params(),
         name="project",
-    )(order, *[pltpu.with_memory_space_constraint(x, pltpu.HBM) for x in row_sets], own, other)
+    )(order, *row_sets, own, other)
 
 
 def unit_sum_kernel(parts_ref, out_ref):
@@ -401,13 +414,10 @@
     owners = low ^ jnp.array([0, 2, 1, 3], jnp.int32)
     outgoing = take_chunks(2 * owners + 1 - core, grad)
     received = flip(outgoing, 1)
-    keep, send = core_sum(2 * owners + core, grad, received)
+    keep, send, units = core_sum(2 * owners + core, grad, received, hidden)
     second_in = flip(send, 2)
 
-    hidden, _ = lax.optimization_barrier((hidden, send))
-    units = jnp.sum(hidden.astype(F32), axis=0).astype(BF16)
-    same = jnp.broadcast_to(units, (4,) + units.shape)
-    same = lax.all_to_all(same, "grp", 0, 0)
+    same = lax.all_to_all(units, "grp", 0, 0)
 
     caches = pack_caches(cache_k, cache_v, cache_scale, fresh_kv, tp % QUADS)
     caches = jnp.broadcast_to(caches, (QUADS,) + caches.shape)
@@ -424,10 +434,10 @@
     two_high = from_plane(same[2:], -2)
     attention = attend(lengths, queries, packed)
 
-    third_in, up, down, two_low, two_high = lax.optimization_barrier(
-        (third_in, up, down, two_low, two_high)
+    codes, own = update(keep, second_in, third_in, master, moment, second)
+    own, up, down, two_low, two_high = lax.optimization_barrier(
+        (own, up, down, two_low, two_high)
     )
-    codes, own = update(keep, second_in, third_in, master, moment, second)
     other = flip(own, 1)
 
     row_at = lax.dynamic_index_in_dim(jnp.array(ROW_AT), plane, 0, keepdims=False)

time: 114 us -> 109 us (0.956)
  the two profiles are of different devices: /device:TPU:116 before, /device:TPU:32 now
where the time goes in v3:
time: 109 us; the launch traced here: 108 us
  starting transfers between devices  55.7 us (51%)
  waiting for transfers between devices  36 us (33%)
  Pallas kernels  9.3 us (9%)
  local copies, waits for them, and re-layouts  4.85 us (4%)
  other arithmetic  1.45 us (1%)
    ppermute x4, starting transfers between devices, from_plane(): lax.ppermute(value, Z, [((d + 2 * ahead) % count, d) for d in range(count)])  14 us
    ppermute x4, starting transfers between devices, flip(): return lax.ppermute(value, 'dp', [(s, s ^ mask) for s in range(8)])  13.1 us
    ppermute x4, waiting for transfers between devices, flip(): return lax.ppermute(value, 'dp', [(s, s ^ mask) for s in range(8)])  10.8 us
    all_to_all x1, starting transfers between devices, shards(): same = lax.all_to_all(units, 'grp', 0, 0)  9.72 us
    all_to_all x1, waiting for transfers between devices, shards(): same = lax.all_to_all(units, 'grp', 0, 0)  9.47 us
    all_to_all x1, starting transfers between devices, shards(): parts = lax.all_to_all(parts, 'tp', 0, 0)  7.91 us
    all_to_all x1, waiting for transfers between devices, shards(): parts = lax.all_to_all(parts, 'tp', 0, 0)  7.6 us
    ppermute x1, starting transfers between devices, shards(): mixed = lax.ppermute(unit_sum(parts), ALL, home_pairs())  7.41 us
  transfers between devices with their start and end apart: 12, of which 7 were waited for; matrix products, arithmetic and copies ran while one was open for 2% of the time, Pallas kernels for 3%

profile of v3, /device:TPU:32, one launch (start us, length us, event | category | flops | bytes accessed | tf_op | source)
XLA Modules:
  0.0 108.2 jit_solution(3579953068742769084)
XLA Ops:
  1.3 1.6 %copy-done = bf16[1,1024,1024]{2,1,0:T(8,128)(2,1)S(1)} copy-done((bf16[1,1024,1024]{2,1,0:T(8,128)(2,1)S(1)}, bf16[1,1024,1024]{2,1,0:T(8,128)(2,1)}, u32[]{:S(2)}) %copy-start) | copy-done | bytes 2097176
  3.9 1.9 %collective-permute-start = (bf16[4,1024,128]{2,1,0:T(8,128)(2,1)S(1)}, bf16[4,1024,128]{2,1,0:T(8,128)(2,1)S(1)}, u32[]{:S(2)}, u32[]{:S(2)}) collective-permute-start(bf16[4,1024,128]{2,1,0:T(8,128)(2,1)S(1)} %take_chunks.1), channel_id=1, source_target_pairs={{0,16},{16,0},{32,48},{48,32},{64,80},{80,64},{96,112},{112,96},{1... | collective-permute-start | bytes 3145736 | tf_op jit(solution)/shard_map/ppermute | solution.py:75
  5.9 2.6 %collective-permute-done.near_in_ref.far_in_ref = bf16[4,1024,128]{2,1,0:T(8,128)(2,1)S(1)} collective-permute-done((bf16[4,1024,128]{2,1,0:T(8,128)(2,1)S(1)}, bf16[4,1024,128]{2,1,0:T(8,128)(2,1)S(1)}, u32[]{:S(2)}, u32[]{:S(2)}) %collective-permute-start) | collective-permute-done | bytes 1048608 | tf_op jit(solution)/shard_map/ppermute | solution.py:75
  8.5 1.9 %core_sum.1 = (bf16[2,1024,128]{2,1,0:T(8,128)(2,1)S(1)}, bf16[2,1024,128]{2,1,0:T(8,128)(2,1)S(1)}, bf16[4,32,1024]{2,1,0:T(8,128)(2,1)}) custom-call(s32[4]{0:T(128)S(1)} %get-tuple-element.29.index_ref, bf16[1024,1024]{1,0:T(8,128)(2,1)S(1)} %bitcast.28, bf16[1024,1024]{1,0:T(8,128)(2,1)S(1)} %bitcast.29, ...), custom_call_target="tpu_custom_call" | custom-call | tf_op jit(solution)/shard_map/core_sum/pallas_call | solution.py:123
  10.4 7.4 %collective-permute-start.1 = (bf16[2,1024,128]{2,1,0:T(8,128)(2,1)S(1)}, bf16[2,1024,128]{2,1,0:T(8,128)(2,1)S(1)}, u32[]{:S(2)}, u32[]{:S(2)}) collective-permute-start(bf16[2,1024,128]{2,1,0:T(8,128)(2,1)S(1)} %get-tuple-element.15), channel_id=1, source_target_pairs={{0,32},{16,48},{32,0},{48,16},{64,96},{80,112},{96,64},{112,80},{1... | collective-permute-start | bytes 1572872 | tf_op jit(solution)/shard_map/ppermute | solution.py:75
  17.7 9.7 %all-to-all-start.1 = ((bf16[4,32,1024]{2,1,0:T(8,128)(2,1)}), bf16[4,32,1024]{2,1,0:T(8,128)(2,1)S(1)}, u32[]{:S(2)}, u32[]{:S(2)}) async-start(bf16[4,32,1024]{2,1,0:T(8,128)(2,1)} %get-tuple-element.18), calls=%async_computation.1 | async-start | bytes 524288 | tf_op jit(solution)/shard_map/all_to_all | solution.py:420
  27.5 7.4 %collective-permute-done.1.received_ref.second_in_ref = bf16[2,1024,128]{2,1,0:T(8,128)(2,1)S(1)} collective-permute-done((bf16[2,1024,128]{2,1,0:T(8,128)(2,1)S(1)}, bf16[2,1024,128]{2,1,0:T(8,128)(2,1)S(1)}, u32[]{:S(2)}, u32[]{:S(2)}) %collective-permute-start.1) | collective-permute-done | bytes 524320 | tf_op jit(solution)/shard_map/ppermute | solution.py:75
  35.7 1.9 %collective-permute-start.2 = (bf16[1024,128]{1,0:T(8,128)(2,1)}, bf16[1024,128]{1,0:T(8,128)(2,1)S(1)}, u32[]{:S(2)}, u32[]{:S(2)}) collective-permute-start(bf16[1024,128]{1,0:T(8,128)(2,1)} %pair_sum.1), channel_id=1, source_target_pairs={{0,64},{16,80},{32,96},{48,112},{64,0},{80,16},{96,32},{112,48},{1... | collective-permute-start | bytes 786440 | tf_op jit(solution)/shard_map/ppermute | solution.py:75
  37.7 9.5 %all-to-all-done.1.same_ref = bf16[4,32,1024]{2,1,0:T(8,128)(2,1)S(1)} async-done(((bf16[4,32,1024]{2,1,0:T(8,128)(2,1)}), bf16[4,32,1024]{2,1,0:T(8,128)(2,1)S(1)}, u32[]{:S(2)}, u32[]{:S(2)}) %all-to-all-start.1) | async-done | bytes 262176 | tf_op jit(solution)/shard_map/all_to_all | solution.py:420
  47.1 5.3 %collective-permute-start.3 = (bf16[4,32,1024]{2,1,0:T(8,128)(2,1)S(1)}, bf16[4,32,1024]{2,1,0:T(8,128)(2,1)S(1)}, u32[]{:S(2)}, u32[]{:S(2)}) collective-permute-start(bf16[4,32,1024]{2,1,0:T(8,128)(2,1)S(1)} %all-to-all-done.1.same_ref), channel_id=1, source_target_pairs={{32,0},{48,16},{64,32},{80,48},{96,64},{112,80},{128,96},{144,112}... | collective-permute-start | bytes 786440 | tf_op jit(solution)/shard_map/ppermute | solution.py:80
  52.5 1.9 %collective-permute-start.4 = (bf16[4,32,1024]{2,1,0:T(8,128)(2,1)S(1)}, bf16[4,32,1024]{2,1,0:T(8,128)(2,1)S(1)}, u32[]{:S(2)}, u32[]{:S(2)}) collective-permute-start(bf16[4,32,1024]{2,1,0:T(8,128)(2,1)S(1)} %all-to-all-done.1.same_ref), channel_id=1, source_target_pairs={{480,0},{496,16},{0,32},{16,48},{32,64},{48,80},{64,96},{80,112},{... | collective-permute-start | bytes 786440 | tf_op jit(solution)/shard_map/ppermute | solution.py:80
  54.4 4.6 %collective-permute-start.5 = (bf16[2,32,1024]{2,1,0:T(8,128)(2,1)S(1)}, bf16[2,32,1024]{2,1,0:T(8,128)(2,1)S(1)}, u32[]{:S(2)}, u32[]{:S(2)}) collective-permute-start(bf16[2,32,1024]{2,1,0:T(8,128)(2,1)S(1)} %get-tuple-element.27), channel_id=1, source_target_pairs={{64,0},{80,16},{96,32},{112,48},{128,64},{144,80},{160,96},{176,11... | collective-permute-start | bytes 393224 | tf_op jit(solution)/shard_map/ppermute | solution.py:80
  59.0 2.2 %collective-permute-start.6 = (bf16[2,32,1024]{2,1,0:T(8,128)(2,1)S(1)}, bf16[2,32,1024]{2,1,0:T(8,128)(2,1)S(1)}, u32[]{:S(2)}, u32[]{:S(2)}) collective-permute-start(bf16[2,32,1024]{2,1,0:T(8,128)(2,1)S(1)} %get-tuple-element.26), channel_id=1, source_target_pairs={{448,0},{464,16},{480,32},{496,48},{0,64},{16,80},{32,96},{48,112}... | collective-permute-start | bytes 393224 | tf_op jit(solution)/shard_map/ppermute | solution.py:80
  62.3 1.0 copy-done.16
  63.3 1.3 %update.1 = (bf16[1024,128]{1,0:T(8,128)(2,1)}, bf16[1152,128]{1,0:T(8,128)(2,1)S(1)}) custom-call(bf16[2,1024,128]{2,1,0:T(8,128)(2,1)S(1)} %copy-done.14, bf16[2,1024,128]{2,1,0:T(8,128)(2,1)S(1)} %copy-done.16, bf16[1024,128]{1,0:T(8,128)(2,1)S(1)} %collective-permute-done.2.third_in_ref, f32[1024,128]{1,0:T(8,128)S(1)} %copy-done.10, ...), custom_call_target="tpu_custom_call" | custom-call | flops 99999997952 | bytes 1000000000 | tf_op jit(solution)/shard_map/update/pallas_call | solution.py:189
  64.7 3.8 %collective-permute-done.6.two_high_ref = bf16[2,32,1024]{2,1,0:T(8,128)(2,1)S(1)} collective-permute-done((bf16[2,32,1024]{2,1,0:T(8,128)(2,1)S(1)}, bf16[2,32,1024]{2,1,0:T(8,128)(2,1)S(1)}, u32[]{:S(2)}, u32[]{:S(2)}) %collective-permute-start.6) | collective-permute-done | bytes 131104 | tf_op jit(solution)/shard_map/ppermute | solution.py:80
  68.5 1.9 %collective-permute-start.7 = (bf16[1152,128]{1,0:T(8,128)(2,1)S(1)}, bf16[1152,128]{1,0:T(8,128)(2,1)S(1)}, u32[]{:S(2)}, u32[]{:S(2)}) collective-permute-start(bf16[1152,128]{1,0:T(8,128)(2,1)S(1)} %get-tuple-element.25.own_ref), channel_id=1, source_target_pairs={{0,16},{16,0},{32,48},{48,32},{64,80},{80,64},{96,112},{112,96},{1... | collective-permute-start | bytes 884744 | tf_op jit(solution)/shard_map/ppermute | solution.py:75
  72.0 2.1 %project.1 = bf16[16,2,32,128]{3,2,1,0:T(8,128)(2,1)} custom-call(s32[17]{0:T(128)S(1)} %pad_add_fusion.order_ref, bf16[4,32,1024]{2,1,0:T(8,128)(2,1)S(1)} %all-to-all-done.1.same_ref, bf16[4,32,1024]{2,1,0:T(8,128)(2,1)S(1)} %collective-permute-done.3.up_ref, bf16[2,32,1024]{2,1,0:T(8,128)(2,1)S(1)} %collective-permute-done.5.two_low_ref, ...), custom_call_target="tpu_custom_call" | custom-call | tf_op jit(solution)/shard_map/project/pallas_call | solution.py:227
  74.1 7.9 %all-to-all-start.2 = ((bf16[16,2,32,128]{3,2,1,0:T(8,128)(2,1)}), bf16[16,2,32,128]{3,2,1,0:T(8,128)(2,1)S(1)}, u32[]{:S(2)}, u32[]{:S(2)}) async-start(bf16[16,2,32,128]{3,2,1,0:T(8,128)(2,1)} %project.1), calls=%async_computation.2 | async-start | bytes 524288 | tf_op jit(solution)/shard_map/all_to_all | solution.py:447
  83.2 7.6 %all-to-all-done.2.parts_ref = bf16[16,2,32,128]{3,2,1,0:T(8,128)(2,1)S(1)} async-done(((bf16[16,2,32,128]{3,2,1,0:T(8,128)(2,1)}), bf16[16,2,32,128]{3,2,1,0:T(8,128)(2,1)S(1)}, u32[]{:S(2)}, u32[]{:S(2)}) %all-to-all-start.2) | async-done | bytes 262176 | tf_op jit(solution)/shard_map/all_to_all | solution.py:447
  90.8 3.5 %all-to-all-start = ((bf16[4,784,128]{2,1,0:T(8,128)(2,1)}), bf16[4,784,128]{2,1,0:T(8,128)(2,1)S(1)}, u32[]{:S(2)}, u32[]{:S(2)}) async-start(bf16[4,784,128]{2,1,0:T(8,128)(2,1)} %broadcast_in_dim.14), calls=%async_computation | async-start | bytes 1605632 | tf_op jit(solution)/shard_map/all_to_all | solution.py:426
  94.4 7.4 %collective-permute-start.8 = (bf16[2,32,128]{2,1,0:T(8,128)(2,1)S(1)}, bf16[2,32,128]{2,1,0:T(8,128)(2,1)S(1)}, u32[]{:S(2)}, u32[]{:S(2)}) collective-permute-start(bf16[2,32,128]{2,1,0:T(8,128)(2,1)S(1)} %unit_sum.1), channel_id=1, source_target_pairs={{10,0},{11,32},{6,64},{13,96},{7,128},{2,160},{4,192},{1,224},{0,2... | collective-permute-start | bytes 49160 | tf_op jit(solution)/shard_map/ppermute | solution.py:448
  101.8 4.3 %all-to-all-done.packed_ref = bf16[4,784,128]{2,1,0:T(8,128)(2,1)S(1)} async-done(((bf16[4,784,128]{2,1,0:T(8,128)(2,1)}), bf16[4,784,128]{2,1,0:T(8,128)(2,1)S(1)}, u32[]{:S(2)}, u32[]{:S(2)}) %all-to-all-start) | async-done | bytes 802848 | tf_op jit(solution)/shard_map/all_to_all | solution.py:426
  106.1 1.4 %attend.1.attention_ref = f32[32,256]{1,0:T(8,128)S(1)} custom-call(s32[1,32]{1,0:T(1,128)S(1)} %bitcast.34, bf16[4,32,256]{2,1,0:T(8,128)(2,1)S(1)} %copy-done.6, bf16[4,784,128]{2,1,0:T(8,128)(2,1)S(1)} %all-to-all-done.packed_ref), custom_call_target="tpu_custom_call" | custom-call | tf_op jit(solution)/shard_map/attend/pallas_call | solution.py:386
  (48 shorter events, 7.0 us)
Async XLA Ops:
  2.9 5.6 %copy-start.2 = (bf16[4,32,1024]{2,1,0:T(8,128)(2,1)S(1)}, bf16[4,32,1024]{2,1,0:T(8,128)(2,1)}, u32[]{:S(2)}) copy-start(bf16[4,32,1024]{2,1,0:T(8,128)(2,1)} %hidden_ref.1) | copy-start | bytes 786436
  3.9 4.6 %collective-permute-start = (bf16[4,1024,128]{2,1,0:T(8,128)(2,1)S(1)}, bf16[4,1024,128]{2,1,0:T(8,128)(2,1)S(1)}, u32[]{:S(2)}, u32[]{:S(2)}) collective-permute-start(bf16[4,1024,128]{2,1,0:T(8,128)(2,1)S(1)} %take_chunks.1), channel_id=1, source_target_pairs={{0,16},{16,0},{32,48},{48,32},{64,80},{80,64},{96,112},{112,96},{1... | collective-permute-start | bytes 3145736 | tf_op jit(solution)/shard_map/ppermute | solution.py:75
  10.4 25.3 %copy-start.13 = (bf16[2,1024,128]{2,1,0:T(8,128)(2,1)}, bf16[2,1024,128]{2,1,0:T(8,128)(2,1)S(1)}, u32[]{:S(2)}) copy-start(bf16[2,1024,128]{2,1,0:T(8,128)(2,1)S(1)} %get-tuple-element.14.keep_ref) | copy-start | bytes 1572868
  10.4 24.5 %collective-permute-start.1 = (bf16[2,1024,128]{2,1,0:T(8,128)(2,1)S(1)}, bf16[2,1024,128]{2,1,0:T(8,128)(2,1)S(1)}, u32[]{:S(2)}, u32[]{:S(2)}) collective-permute-start(bf16[2,1024,128]{2,1,0:T(8,128)(2,1)S(1)} %get-tuple-element.15), channel_id=1, source_target_pairs={{0,32},{16,48},{32,0},{48,16},{64,96},{80,112},{96,64},{112,80},{1... | collective-permute-start | bytes 1572872 | tf_op jit(solution)/shard_map/ppermute | solution.py:75
  17.7 29.4 %all-to-all-start.1 = ((bf16[4,32,1024]{2,1,0:T(8,128)(2,1)}), bf16[4,32,1024]{2,1,0:T(8,128)(2,1)S(1)}, u32[]{:S(2)}, u32[]{:S(2)}) async-start(bf16[4,32,1024]{2,1,0:T(8,128)(2,1)} %get-tuple-element.18), calls=%async_computation.1 | async-start | bytes 524288 | tf_op jit(solution)/shard_map/all_to_all | solution.py:420
  34.8 26.4 %copy-start.10 = (f32[1024,128]{1,0:T(8,128)S(1)}, f32[1024,128]{1,0:T(8,128)}, u32[]{:S(2)}) copy-start(f32[1024,128]{1,0:T(8,128)} %master_ref.1) | copy-start | bytes 1572868
  34.9 26.4 %copy-start.11 = (f32[1024,128]{1,0:T(8,128)S(1)}, f32[1024,128]{1,0:T(8,128)}, u32[]{:S(2)}) copy-start(f32[1024,128]{1,0:T(8,128)} %moment_ref.1) | copy-start | bytes 1572868
  34.9 26.4 %copy-start.12 = (f32[1024,128]{1,0:T(8,128)S(1)}, f32[1024,128]{1,0:T(8,128)}, u32[]{:S(2)}) copy-start(f32[1024,128]{1,0:T(8,128)} %second_ref.1) | copy-start | bytes 1572868
  35.7 25.5 %collective-permute-start.2 = (bf16[1024,128]{1,0:T(8,128)(2,1)}, bf16[1024,128]{1,0:T(8,128)(2,1)S(1)}, u32[]{:S(2)}, u32[]{:S(2)}) collective-permute-start(bf16[1024,128]{1,0:T(8,128)(2,1)} %pair_sum.1), channel_id=1, source_target_pairs={{0,64},{16,80},{32,96},{48,112},{64,0},{80,16},{96,32},{112,48},{1... | collective-permute-start | bytes 786440 | tf_op jit(solution)/shard_map/ppermute | solution.py:75
  47.1 21.4 %collective-permute-start.3 = (bf16[4,32,1024]{2,1,0:T(8,128)(2,1)S(1)}, bf16[4,32,1024]{2,1,0:T(8,128)(2,1)S(1)}, u32[]{:S(2)}, u32[]{:S(2)}) collective-permute-start(bf16[4,32,1024]{2,1,0:T(8,128)(2,1)S(1)} %all-to-all-done.1.same_ref), channel_id=1, source_target_pairs={{32,0},{48,16},{64,32},{80,48},{96,64},{112,80},{128,96},{144,112}... | collective-permute-start | bytes 786440 | tf_op jit(solution)/shard_map/ppermute | solution.py:80
  52.5 16.0 %collective-permute-start.4 = (bf16[4,32,1024]{2,1,0:T(8,128)(2,1)S(1)}, bf16[4,32,1024]{2,1,0:T(8,128)(2,1)S(1)}, u32[]{:S(2)}, u32[]{:S(2)}) collective-permute-start(bf16[4,32,1024]{2,1,0:T(8,128)(2,1)S(1)} %all-to-all-done.1.same_ref), channel_id=1, source_target_pairs={{480,0},{496,16},{0,32},{16,48},{32,64},{48,80},{64,96},{80,112},{... | collective-permute-start | bytes 786440 | tf_op jit(solution)/shard_map/ppermute | solution.py:80
  54.4 10.2 %collective-permute-start.5 = (bf16[2,32,1024]{2,1,0:T(8,128)(2,1)S(1)}, bf16[2,32,1024]{2,1,0:T(8,128)(2,1)S(1)}, u32[]{:S(2)}, u32[]{:S(2)}) collective-permute-start(bf16[2,32,1024]{2,1,0:T(8,128)(2,1)S(1)} %get-tuple-element.27), channel_id=1, source_target_pairs={{64,0},{80,16},{96,32},{112,48},{128,64},{144,80},{160,96},{176,11... | collective-permute-start | bytes 393224 | tf_op jit(solution)/shard_map/ppermute | solution.py:80
  59.0 9.5 %collective-permute-start.6 = (bf16[2,32,1024]{2,1,0:T(8,128)(2,1)S(1)}, bf16[2,32,1024]{2,1,0:T(8,128)(2,1)S(1)}, u32[]{:S(2)}, u32[]{:S(2)}) collective-permute-start(bf16[2,32,1024]{2,1,0:T(8,128)(2,1)S(1)} %get-tuple-element.26), channel_id=1, source_target_pairs={{448,0},{464,16},{480,32},{496,48},{0,64},{16,80},{32,96},{48,112}... | collective-permute-start | bytes 393224 | tf_op jit(solution)/shard_map/ppermute | solution.py:80
  64.6 17.4 %copy-start.3 = (bf16[32,8,128]{2,1,0:T(8,128)(2,1)S(1)}, bf16[32,8,128]{2,1,0:T(8,128)(2,1)}, u32[]{:S(2)}) copy-start(bf16[32,8,128]{2,1,0:T(8,128)(2,1)} %param.22) | copy-start | bytes 196612
  64.6 17.4 %copy-start.4 = (bf16[32,8,128]{2,1,0:T(8,128)(2,1)S(1)}, bf16[32,8,128]{2,1,0:T(8,128)(2,1)}, u32[]{:S(2)}) copy-start(bf16[32,8,128]{2,1,0:T(8,128)(2,1)} %param.23) | copy-start | bytes 196612
  64.6 17.4 %copy-start.5 = (bf16[4,32,2,32]{3,2,1,0:T(2,128)(2,1)S(1)}, bf16[4,32,2,32]{3,2,1,0:T(2,128)(2,1)}, u32[]{:S(2)}) copy-start(bf16[4,32,2,32]{3,2,1,0:T(2,128)(2,1)} %param.21) | copy-start | bytes 49156
  64.6 17.4 %copy-start.8 = (bf16[32,2,8]{0,2,1:T(8,128)(2,1)S(1)}, bf16[32,2,8]{0,2,1:T(8,128)(2,1)}, u32[]{:S(2)}) copy-start(bf16[32,2,8]{0,2,1:T(8,128)(2,1)} %param.24) | copy-start | bytes 3076
  68.5 3.5 %collective-permute-start.7 = (bf16[1152,128]{1,0:T(8,128)(2,1)S(1)}, bf16[1152,128]{1,0:T(8,128)(2,1)S(1)}, u32[]{:S(2)}, u32[]{:S(2)}) collective-permute-start(bf16[1152,128]{1,0:T(8,128)(2,1)S(1)} %get-tuple-element.25.own_ref), channel_id=1, source_target_pairs={{0,16},{16,0},{32,48},{48,32},{64,80},{80,64},{96,112},{112,96},{1... | collective-permute-start | bytes 884744 | tf_op jit(solution)/shard_map/ppermute | solution.py:75
  74.1 32.0 %copy-start.6 = (bf16[4,32,256]{2,1,0:T(8,128)(2,1)S(1)}, bf16[4,32,256]{2,1,0:T(8,128)(2,1)}, u32[]{:S(2)}) copy-start(bf16[4,32,256]{2,1,0:T(8,128)(2,1)} %queries_ref.1) | copy-start | bytes 196612
  74.1 32.0 %copy-start.9 = (s32[32]{0:T(128)S(1)}, s32[32]{0:T(128)}, u32[]{:S(2)}) copy-start(s32[32]{0:T(128)} %param.25) | copy-start | bytes 388
  74.1 16.7 %all-to-all-start.2 = ((bf16[16,2,32,128]{3,2,1,0:T(8,128)(2,1)}), bf16[16,2,32,128]{3,2,1,0:T(8,128)(2,1)S(1)}, u32[]{:S(2)}, u32[]{:S(2)}) async-start(bf16[16,2,32,128]{3,2,1,0:T(8,128)(2,1)} %project.1), calls=%async_computation.2 | async-start | bytes 524288 | tf_op jit(solution)/shard_map/all_to_all | solution.py:447
  82.0 25.5 %copy-start.7 = (bf16[32,256]{1,0:T(8,128)(2,1)S(1)}, bf16[32,256]{1,0:T(8,128)(2,1)}, u32[]{:S(2)}) copy-start(bf16[32,256]{1,0:T(8,128)(2,1)} %state_ref.1) | copy-start | bytes 49156
  90.8 15.3 %all-to-all-start = ((bf16[4,784,128]{2,1,0:T(8,128)(2,1)}), bf16[4,784,128]{2,1,0:T(8,128)(2,1)S(1)}, u32[]{:S(2)}, u32[]{:S(2)}) async-start(bf16[4,784,128]{2,1,0:T(8,128)(2,1)} %broadcast_in_dim.14), calls=%async_computation | async-start | bytes 1605632 | tf_op jit(solution)/shard_map/all_to_all | solution.py:426
  94.4 13.1 %collective-permute-start.8 = (bf16[2,32,128]{2,1,0:T(8,128)(2,1)S(1)}, bf16[2,32,128]{2,1,0:T(8,128)(2,1)S(1)}, u32[]{:S(2)}, u32[]{:S(2)}) collective-permute-start(bf16[2,32,128]{2,1,0:T(8,128)(2,1)S(1)} %unit_sum.1), channel_id=1, source_target_pairs={{10,0},{11,32},{6,64},{13,96},{7,128},{2,160},{4,192},{1,224},{0,2... | collective-permute-start | bytes 49160 | tf_op jit(solution)/shard_map/ppermute | solution.py:448
  (5 other events, 10.1 us)

commit v4 on v3

--- a/solution.py
+++ b/solution.py
@@ -76,8 +76,16 @@
 
 
 def from_plane(value, ahead):
-    count = 2 * CHIPS
-    return lax.ppermute(value, Z, [((d + 2 * ahead) % count, d) for d in range(count)])
+    pairs = [
+        ((plane + ahead(plane)) % CHIPS * 2 + core, plane * 2 + core)
+        for plane in range(CHIPS)
+        for core in range(2)
+    ]
+    return lax.ppermute(value, Z, pairs)
+
+
+def swap(value, mask):
+    return lax.ppermute(value, "tp", [(s, s ^ mask) for s in range(CHIPS)])
 
 
 def split_kernel(index_ref, grad_ref, out_ref):
@@ -201,10 +209,12 @@
     )(keep, second_in, third_in, master, moment, second)
 
 
-def project_kernel(order_ref, same_ref, up_ref, two_low_ref, two_high_ref, down_ref, own_ref, other_ref, out_ref, sums):
+def project_kernel(
+    order_ref, same_ref, up_ref, two_ref, down_ref, own_ref, other_ref, out_ref, sums
+):
     core = order_ref[CHIPS]
     start = 0
-    for rows_ref in (same_ref, up_ref, two_low_ref, two_high_ref, down_ref):
+    for rows_ref in (same_ref, up_ref, two_ref, down_ref):
         count = rows_ref.shape[0]
         for which, codes_ref in enumerate((own_ref, other_ref)):
             total = jnp.zeros((count * ROWS, BLK), F32)
@@ -319,23 +329,24 @@
     )
 
 
-def attend_kernel(lengths_ref, queries_ref, packed_ref, out_ref):
+def attend_kernel(place_ref, lengths_ref, queries_ref, *refs):
+    packed_refs, out_ref = refs[:QUADS], refs[QUADS]
     inv = 1.0 / math.sqrt(HD)
     slots = QUADS * KEYS
-    keys = packed_ref[:, :KEYS].reshape(slots, HD)
-    values = packed_ref[:, KEYS : 2 * KEYS].reshape(slots, HD)
-    fresh = packed_ref[0, 2 * KEYS : SCALES_AT].astype(F32)
-    for place in range(1, QUADS):
-        fresh = fresh + packed_ref[place, 2 * KEYS : SCALES_AT].astype(F32)
+    keys = jnp.concatenate([ref[:KEYS] for ref in packed_refs], axis=0)
+    values = jnp.concatenate([ref[KEYS : 2 * KEYS] for ref in packed_refs], axis=0)
+    fresh = packed_refs[0][2 * KEYS : SCALES_AT].astype(F32)
+    for ref in packed_refs[1:]:
+        fresh = fresh + ref[2 * KEYS : SCALES_AT].astype(F32)
     new_keys = fresh.astype(BF16)
     new_values = pltpu.roll(fresh, FRESH - 1, 0).astype(BF16)
-    scales = packed_ref[:, SCALES_AT:].astype(F32)
+    scales = [ref[SCALES_AT:].astype(F32) for ref in packed_refs]
     lines = KEYS // HD
     key_scale = jnp.concatenate(
-        [scales[p, i : i + 1] for p in range(QUADS) for i in range(lines)], axis=1
+        [scales[p][i : i + 1] for p in range(QUADS) for i in range(lines)], axis=1
     )
     value_scale = jnp.concatenate(
-        [scales[p, lines + i : lines + i + 1] for p in range(QUADS) for i in range(lines)], axis=1
+        [scales[p][lines + i : lines + i + 1] for p in range(QUADS) for i in range(lines)], axis=1
     )
     row = lax.broadcasted_iota(jnp.int32, (ROWS, ROWS), 0)
     column = lax.broadcasted_iota(jnp.int32, (ROWS, ROWS), 1)
@@ -343,7 +354,7 @@
     length = jnp.sum(length, axis=1, keepdims=True).astype(jnp.int32)
     lane = lax.broadcasted_iota(jnp.int32, (ROWS, slots), 1)
     row = lax.broadcasted_iota(jnp.int32, (ROWS, slots), 0)
-    slot = (lane // KEYS) * SLOTS + (lane & (SLOTS - 1))
+    slot = ((lane // KEYS) ^ place_ref[0]) * SLOTS + (lane & (SLOTS - 1))
     live = ((lane // SLOTS) & (ROWS - 1)) == row
     live = live & (slot < length)
     ahead = slot - length
@@ -382,13 +393,16 @@
         ) + jnp.dot(new, new_values, preferred_element_type=F32)
 
 
-def attend(lengths, queries, packed):
+def attend(place, lengths, queries, packed):
+    vmem = pl.BlockSpec(memory_space=pltpu.VMEM)
     return pl.pallas_call(
         attend_kernel,
+        in_specs=[pl.BlockSpec(memory_space=pltpu.SMEM)] + [vmem] * (2 + QUADS),
+        out_specs=vmem,
         out_shape=jax.ShapeDtypeStruct((ROWS, 2 * HD), F32),
         compiler_params=params(),
         name="attend",
-    )(lengths[None], queries, packed)
+    )(place[None], lengths[None], queries, *packed)
 
 
 def shards(
@@ -419,31 +433,28 @@
 
     same = lax.all_to_all(units, "grp", 0, 0)
 
-    caches = pack_caches(cache_k, cache_v, cache_scale, fresh_kv, tp % QUADS)
-    caches = jnp.broadcast_to(caches, (QUADS,) + caches.shape)
-    caches, _ = lax.optimization_barrier((caches, send))
-    quads = [[QUADS * x + y for y in range(QUADS)] for x in range(QUADS)]
-    packed = lax.all_to_all(caches, "tp", 0, 0, axis_index_groups=quads)
-
     third = pair_sum(keep, second_in)
     third_in = flip(third, 4)
     same, _ = lax.optimization_barrier((same, third))
-    up = from_plane(same, 1)
-    down = from_plane(same, -1)
-    two_low = from_plane(same[:2], 2)
-    two_high = from_plane(same[2:], -2)
-    attention = attend(lengths, queries, packed)
+    place = tp % QUADS
+    caches = pack_caches(cache_k, cache_v, cache_scale, fresh_kv, place)
+    caches, _, _ = lax.optimization_barrier((caches, third, same))
+    first = swap(caches, 1)
+    two = from_plane(same, lambda plane: 2 if plane % 2 == 0 else -2)
+    up = from_plane(same, lambda plane: 1)
+    down = from_plane(same, lambda plane: -1)
 
     codes, own = update(keep, second_in, third_in, master, moment, second)
-    own, up, down, two_low, two_high = lax.optimization_barrier(
-        (own, up, down, two_low, two_high)
-    )
+    own, two, up, down, first = lax.optimization_barrier((own, two, up, down, first))
     other = flip(own, 1)
 
     row_at = lax.dynamic_index_in_dim(jnp.array(ROW_AT), plane, 0, keepdims=False)
     order = ((row_at - low) & 3) * 4 + row_at // 4
     order = jnp.concatenate([order, core[None]]).astype(jnp.int32)
-    parts = project(order, (same, up, two_low, two_high, down), own, other)
+    parts = project(order, (same, up, two, down), own, other)
+    caches, parts = lax.optimization_barrier((caches, parts))
+    packed = [caches, first] + [swap(caches, mask) for mask in range(2, QUADS)]
+    attention = attend(place, lengths, queries, packed)
     parts = lax.all_to_all(parts, "tp", 0, 0)
     mixed = lax.ppermute(unit_sum(parts), ALL, home_pairs())
     return (codes, finish(state, attention, mixed))

time: 109 us -> 103 us (0.945)
  the two profiles are of different devices: /device:TPU:32 before, /device:TPU:4 now
where the time goes in v4:
time: 103 us
  starting transfers between devices  59 us (57%)
  waiting for transfers between devices  27.3 us (27%)
  Pallas kernels  9.17 us (9%)
  local copies, waits for them, and re-layouts  4.82 us (5%)
  other arithmetic  1.45 us (1%)
    all_to_all x1, waiting for transfers between devices, shards(): same = lax.all_to_all(units, 'grp', 0, 0)  18.2 us
    all_to_all x1, starting transfers between devices, shards(): same = lax.all_to_all(units, 'grp', 0, 0)  14.2 us
    ppermute x3, starting transfers between devices, swap(): return lax.ppermute(value, 'tp', [(s, s ^ mask) for s in range(CHIPS)])  11.4 us
    ppermute x4, starting transfers between devices, flip(): return lax.ppermute(value, 'dp', [(s, s ^ mask) for s in range(8)])  11.2 us
    ppermute x3, starting transfers between devices, from_plane(): return lax.ppermute(value, Z, pairs)  7.89 us
    ppermute x1, starting transfers between devices, shards(): mixed = lax.ppermute(unit_sum(parts), ALL, home_pairs())  7.18 us
    all_to_all x1, starting transfers between devices, shards(): parts = lax.all_to_all(parts, 'tp', 0, 0)  7.16 us
    ppermute x1, waiting for transfers between devices, shards(): mixed = lax.ppermute(unit_sum(parts), ALL, home_pairs())  5.64 us
  transfers between devices with their start and end apart: 13, of which 5 were waited for; matrix products, arithmetic and copies ran while one was open for 1% of the time, Pallas kernels for 4%

profile of v4, /device:TPU:4, one launch (start us, length us, event | category | flops | bytes accessed | tf_op | source)
XLA Modules:
  0.0 102.7 jit_solution(16544718565842171722)
XLA Ops:
  1.3 1.6 %copy-done = bf16[1,1024,1024]{2,1,0:T(8,128)(2,1)S(1)} copy-done((bf16[1,1024,1024]{2,1,0:T(8,128)(2,1)S(1)}, bf16[1,1024,1024]{2,1,0:T(8,128)(2,1)}, u32[]{:S(2)}) %copy-start) | copy-done | bytes 2097176
  3.9 1.9 %collective-permute-start = (bf16[4,1024,128]{2,1,0:T(8,128)(2,1)S(1)}, bf16[4,1024,128]{2,1,0:T(8,128)(2,1)S(1)}, u32[]{:S(2)}, u32[]{:S(2)}) collective-permute-start(bf16[4,1024,128]{2,1,0:T(8,128)(2,1)S(1)} %take_chunks.1), channel_id=1, source_target_pairs={{0,16},{16,0},{32,48},{48,32},{64,80},{80,64},{96,112},{112,96},{1... | collective-permute-start | bytes 3145736 | tf_op jit(solution)/shard_map/ppermute | solution.py:75
  5.9 2.6 %collective-permute-done.near_in_ref.far_in_ref = bf16[4,1024,128]{2,1,0:T(8,128)(2,1)S(1)} collective-permute-done((bf16[4,1024,128]{2,1,0:T(8,128)(2,1)S(1)}, bf16[4,1024,128]{2,1,0:T(8,128)(2,1)S(1)}, u32[]{:S(2)}, u32[]{:S(2)}) %collective-permute-start) | collective-permute-done | bytes 1048608 | tf_op jit(solution)/shard_map/ppermute | solution.py:75
  8.5 1.9 %core_sum.1 = (bf16[2,1024,128]{2,1,0:T(8,128)(2,1)S(1)}, bf16[2,1024,128]{2,1,0:T(8,128)(2,1)S(1)}, bf16[4,32,1024]{2,1,0:T(8,128)(2,1)}) custom-call(s32[4]{0:T(128)S(1)} %get-tuple-element.31.index_ref, bf16[1024,1024]{1,0:T(8,128)(2,1)S(1)} %bitcast.28, bf16[1024,1024]{1,0:T(8,128)(2,1)S(1)} %bitcast.29, ...), custom_call_target="tpu_custom_call" | custom-call | tf_op jit(solution)/shard_map/core_sum/pallas_call | solution.py:131
  10.4 3.8 %collective-permute-start.1 = (bf16[2,1024,128]{2,1,0:T(8,128)(2,1)S(1)}, bf16[2,1024,128]{2,1,0:T(8,128)(2,1)S(1)}, u32[]{:S(2)}, u32[]{:S(2)}) collective-permute-start(bf16[2,1024,128]{2,1,0:T(8,128)(2,1)S(1)} %get-tuple-element.17), channel_id=1, source_target_pairs={{0,32},{16,48},{32,0},{48,16},{64,96},{80,112},{96,64},{112,80},{1... | collective-permute-start | bytes 1572872 | tf_op jit(solution)/shard_map/ppermute | solution.py:75
  14.2 14.2 %all-to-all-start = ((bf16[4,32,1024]{2,1,0:T(8,128)(2,1)}), bf16[4,32,1024]{2,1,0:T(8,128)(2,1)S(1)}, u32[]{:S(2)}, u32[]{:S(2)}) async-start(bf16[4,32,1024]{2,1,0:T(8,128)(2,1)} %get-tuple-element.19), calls=%async_computation | async-start | bytes 524288 | tf_op jit(solution)/shard_map/all_to_all | solution.py:434
  29.3 3.4 %collective-permute-start.2 = (bf16[1024,128]{1,0:T(8,128)(2,1)}, bf16[1024,128]{1,0:T(8,128)(2,1)S(1)}, u32[]{:S(2)}, u32[]{:S(2)}) collective-permute-start(bf16[1024,128]{1,0:T(8,128)(2,1)} %pair_sum.1), channel_id=1, source_target_pairs={{0,64},{16,80},{32,96},{48,112},{64,0},{80,16},{96,32},{112,48},{1... | collective-permute-start | bytes 786440 | tf_op jit(solution)/shard_map/ppermute | solution.py:75
  32.8 18.2 %all-to-all-done.same_ref = bf16[4,32,1024]{2,1,0:T(8,128)(2,1)S(1)} async-done(((bf16[4,32,1024]{2,1,0:T(8,128)(2,1)}), bf16[4,32,1024]{2,1,0:T(8,128)(2,1)S(1)}, u32[]{:S(2)}, u32[]{:S(2)}) %all-to-all-start) | async-done | bytes 262176 | tf_op jit(solution)/shard_map/all_to_all | solution.py:434
  51.0 2.0 %collective-permute-start.3 = (bf16[4,32,1024]{2,1,0:T(8,128)(2,1)S(1)}, bf16[4,32,1024]{2,1,0:T(8,128)(2,1)S(1)}, u32[]{:S(2)}, u32[]{:S(2)}) collective-permute-start(bf16[4,32,1024]{2,1,0:T(8,128)(2,1)S(1)} %all-to-all-done.same_ref), channel_id=1, source_target_pairs={{64,0},{80,16},{480,32},{496,48},{128,64},{144,80},{32,96},{48,112... | collective-permute-start | bytes 786440 | tf_op jit(solution)/shard_map/ppermute | solution.py:84
  53.1 2.1 %collective-permute-start.4 = (bf16[4,32,1024]{2,1,0:T(8,128)(2,1)S(1)}, bf16[4,32,1024]{2,1,0:T(8,128)(2,1)S(1)}, u32[]{:S(2)}, u32[]{:S(2)}) collective-permute-start(bf16[4,32,1024]{2,1,0:T(8,128)(2,1)S(1)} %all-to-all-done.same_ref), channel_id=1, source_target_pairs={{32,0},{48,16},{64,32},{80,48},{96,64},{112,80},{128,96},{144,112}... | collective-permute-start | bytes 786440 | tf_op jit(solution)/shard_map/ppermute | solution.py:84
  55.1 3.8 %collective-permute-start.5 = (bf16[4,32,1024]{2,1,0:T(8,128)(2,1)S(1)}, bf16[4,32,1024]{2,1,0:T(8,128)(2,1)S(1)}, u32[]{:S(2)}, u32[]{:S(2)}) collective-permute-start(bf16[4,32,1024]{2,1,0:T(8,128)(2,1)S(1)} %all-to-all-done.same_ref), channel_id=1, source_target_pairs={{480,0},{496,16},{0,32},{16,48},{32,64},{48,80},{64,96},{80,112},{... | collective-permute-start | bytes 786440 | tf_op jit(solution)/shard_map/ppermute | solution.py:84
  58.9 3.5 %collective-permute-start.6 = (bf16[784,128]{1,0:T(8,128)(2,1)S(1)}, bf16[784,128]{1,0:T(8,128)(2,1)S(1)}, u32[]{:S(2)}, u32[]{:S(2)}) collective-permute-start(bf16[784,128]{1,0:T(8,128)(2,1)S(1)} %pack_caches.1.refs_0_), channel_id=1, source_target_pairs={{0,1},{1,0},{2,3},{3,2},{4,5},{5,4},{6,7},{7,6},{8,9},{9,8},{10,11... | collective-permute-start | bytes 602120 | tf_op jit(solution)/shard_map/ppermute | solution.py:88
  62.5 1.0 %copy-done.12 = f32[1024,128]{1,0:T(8,128)S(1)} copy-done((f32[1024,128]{1,0:T(8,128)S(1)}, f32[1024,128]{1,0:T(8,128)}, u32[]{:S(2)}) %copy-start.12) | copy-done | bytes 524312
  63.5 1.0 %copy-done.14 = bf16[2,1024,128]{2,1,0:T(8,128)(2,1)S(1)} copy-done((bf16[2,1024,128]{2,1,0:T(8,128)(2,1)S(1)}, bf16[2,1024,128]{2,1,0:T(8,128)(2,1)}, u32[]{:S(2)}) %copy-start.14) | copy-done | bytes 524312
  64.5 1.0 %copy-done.16 = bf16[2,1024,128]{2,1,0:T(8,128)(2,1)S(1)} copy-done((bf16[2,1024,128]{2,1,0:T(8,128)(2,1)S(1)}, bf16[2,1024,128]{2,1,0:T(8,128)(2,1)}, u32[]{:S(2)}) %copy-start.16) | copy-done | bytes 524312
  65.6 1.3 %update.1 = (bf16[1024,128]{1,0:T(8,128)(2,1)}, bf16[1152,128]{1,0:T(8,128)(2,1)S(1)}) custom-call(bf16[2,1024,128]{2,1,0:T(8,128)(2,1)S(1)} %copy-done.14, bf16[2,1024,128]{2,1,0:T(8,128)(2,1)S(1)} %copy-done.16, bf16[1024,128]{1,0:T(8,128)(2,1)S(1)} %collective-permute-done.2.third_in_ref, f32[1024,128]{1,0:T(8,128)S(1)} %copy-done.10, ...), custom_call_target="tpu_custom_call" | custom-call | flops 99999997952 | bytes 1000000000 | tf_op jit(solution)/shard_map/update/pallas_call | solution.py:197
  67.0 2.1 %collective-permute-start.7 = (bf16[1152,128]{1,0:T(8,128)(2,1)S(1)}, bf16[1152,128]{1,0:T(8,128)(2,1)S(1)}, u32[]{:S(2)}, u32[]{:S(2)}) collective-permute-start(bf16[1152,128]{1,0:T(8,128)(2,1)S(1)} %get-tuple-element.26.own_ref), channel_id=1, source_target_pairs={{0,16},{16,0},{32,48},{48,32},{64,80},{80,64},{96,112},{112,96},{1... | collective-permute-start | bytes 884744 | tf_op jit(solution)/shard_map/ppermute | solution.py:75
  70.6 2.0 %project.1 = bf16[16,2,32,128]{3,2,1,0:T(8,128)(2,1)} custom-call(s32[17]{0:T(128)S(1)} %pad_add_fusion.order_ref, bf16[4,32,1024]{2,1,0:T(8,128)(2,1)S(1)} %all-to-all-done.same_ref, bf16[4,32,1024]{2,1,0:T(8,128)(2,1)S(1)} %collective-permute-done.4.up_ref, bf16[4,32,1024]{2,1,0:T(8,128)(2,1)S(1)} %collective-permute-done.3.two_ref, ...), custom_call_target="tpu_custom_call" | custom-call | tf_op jit(solution)/shard_map/project/pallas_call | solution.py:237
  72.5 7.2 %all-to-all-start.1 = ((bf16[16,2,32,128]{3,2,1,0:T(8,128)(2,1)}), bf16[16,2,32,128]{3,2,1,0:T(8,128)(2,1)S(1)}, u32[]{:S(2)}, u32[]{:S(2)}) async-start(bf16[16,2,32,128]{3,2,1,0:T(8,128)(2,1)} %project.1), calls=%async_computation.1 | async-start | bytes 524288 | tf_op jit(solution)/shard_map/all_to_all | solution.py:458
  79.7 4.9 %collective-permute-start.8 = (bf16[784,128]{1,0:T(8,128)(2,1)S(1)}, bf16[784,128]{1,0:T(8,128)(2,1)S(1)}, u32[]{:S(2)}, u32[]{:S(2)}) collective-permute-start(bf16[784,128]{1,0:T(8,128)(2,1)S(1)} %pack_caches.1.refs_0_), channel_id=1, source_target_pairs={{0,2},{1,3},{2,0},{3,1},{4,6},{5,7},{6,4},{7,5},{8,10},{9,11},{10,... | collective-permute-start | bytes 602120 | tf_op jit(solution)/shard_map/ppermute | solution.py:88
  84.6 3.1 %collective-permute-start.9 = (bf16[784,128]{1,0:T(8,128)(2,1)S(1)}, bf16[784,128]{1,0:T(8,128)(2,1)S(1)}, u32[]{:S(2)}, u32[]{:S(2)}) collective-permute-start(bf16[784,128]{1,0:T(8,128)(2,1)S(1)} %pack_caches.1.refs_0_), channel_id=1, source_target_pairs={{0,3},{1,2},{2,1},{3,0},{4,7},{5,6},{6,5},{7,4},{8,11},{9,10},{10,... | collective-permute-start | bytes 602120 | tf_op jit(solution)/shard_map/ppermute | solution.py:88
  87.7 7.2 %collective-permute-start.10 = (bf16[2,32,128]{2,1,0:T(8,128)(2,1)S(1)}, bf16[2,32,128]{2,1,0:T(8,128)(2,1)S(1)}, u32[]{:S(2)}, u32[]{:S(2)}) collective-permute-start(bf16[2,32,128]{2,1,0:T(8,128)(2,1)S(1)} %unit_sum.1), channel_id=1, source_target_pairs={{10,0},{11,32},{6,64},{13,96},{7,128},{2,160},{4,192},{1,224},{0,2... | collective-permute-start | bytes 49160 | tf_op jit(solution)/shard_map/ppermute | solution.py:459
  95.0 1.4 %attend.1.attention_ref = f32[32,256]{1,0:T(8,128)S(1)} custom-call(s32[1]{0:T(128)} %bitcast.1.place_ref, s32[1,32]{1,0:T(1,128)S(1)} %bitcast.34, bf16[4,32,256]{2,1,0:T(8,128)(2,1)S(1)} %copy-done.6, bf16[784,128]{1,0:T(8,128)(2,1)S(1)} %pack_caches.1.refs_0_, bf16[784,128]{1,0:T(8,128)(2,1)S(1)} %collective-permute-done.6.refs_1_, ...), custom_call_target="tpu_custom_call" | custom-call | tf_op jit(solution)/shard_map/attend/pallas_call | solution.py:398
  96.4 5.6 %collective-permute-done.10.mixed_ref = bf16[2,32,128]{2,1,0:T(8,128)(2,1)S(1)} collective-permute-done((bf16[2,32,128]{2,1,0:T(8,128)(2,1)S(1)}, bf16[2,32,128]{2,1,0:T(8,128)(2,1)S(1)}, u32[]{:S(2)}, u32[]{:S(2)}) %collective-permute-start.10) | collective-permute-done | bytes 16416 | tf_op jit(solution)/shard_map/ppermute | solution.py:459
  (48 shorter events, 5.0 us)
Async XLA Ops:
  2.9 5.6 %copy-start.1 = (bf16[1,1024,1024]{2,1,0:T(8,128)(2,1)S(1)}, bf16[1,1024,1024]{2,1,0:T(8,128)(2,1)}, u32[]{:S(2)}) copy-start(bf16[1,1024,1024]{2,1,0:T(8,128)(2,1)} %param.14) | copy-start | bytes 6291460
  2.9 5.6 %copy-start.2 = (bf16[4,32,1024]{2,1,0:T(8,128)(2,1)S(1)}, bf16[4,32,1024]{2,1,0:T(8,128)(2,1)}, u32[]{:S(2)}) copy-start(bf16[4,32,1024]{2,1,0:T(8,128)(2,1)} %hidden_ref.1) | copy-start | bytes 786436
  3.9 4.6 %collective-permute-start = (bf16[4,1024,128]{2,1,0:T(8,128)(2,1)S(1)}, bf16[4,1024,128]{2,1,0:T(8,128)(2,1)S(1)}, u32[]{:S(2)}, u32[]{:S(2)}) collective-permute-start(bf16[4,1024,128]{2,1,0:T(8,128)(2,1)S(1)} %take_chunks.1), channel_id=1, source_target_pairs={{0,16},{16,0},{32,48},{48,32},{64,80},{80,64},{96,112},{112,96},{1... | collective-permute-start | bytes 3145736 | tf_op jit(solution)/shard_map/ppermute | solution.py:75
  10.4 18.9 %copy-start.13 = (bf16[2,1024,128]{2,1,0:T(8,128)(2,1)}, bf16[2,1024,128]{2,1,0:T(8,128)(2,1)S(1)}, u32[]{:S(2)}) copy-start(bf16[2,1024,128]{2,1,0:T(8,128)(2,1)S(1)} %get-tuple-element.16.keep_ref) | copy-start | bytes 1572868
  10.4 18.0 %collective-permute-start.1 = (bf16[2,1024,128]{2,1,0:T(8,128)(2,1)S(1)}, bf16[2,1024,128]{2,1,0:T(8,128)(2,1)S(1)}, u32[]{:S(2)}, u32[]{:S(2)}) collective-permute-start(bf16[2,1024,128]{2,1,0:T(8,128)(2,1)S(1)} %get-tuple-element.17), channel_id=1, source_target_pairs={{0,32},{16,48},{32,0},{48,16},{64,96},{80,112},{96,64},{112,80},{1... | collective-permute-start | bytes 1572872 | tf_op jit(solution)/shard_map/ppermute | solution.py:75
  14.2 36.8 %all-to-all-start = ((bf16[4,32,1024]{2,1,0:T(8,128)(2,1)}), bf16[4,32,1024]{2,1,0:T(8,128)(2,1)S(1)}, u32[]{:S(2)}, u32[]{:S(2)}) async-start(bf16[4,32,1024]{2,1,0:T(8,128)(2,1)} %get-tuple-element.19), calls=%async_computation | async-start | bytes 524288 | tf_op jit(solution)/shard_map/all_to_all | solution.py:434
  28.4 4.3 %copy-start.3 = (bf16[32,8,128]{2,1,0:T(8,128)(2,1)S(1)}, bf16[32,8,128]{2,1,0:T(8,128)(2,1)}, u32[]{:S(2)}) copy-start(bf16[32,8,128]{2,1,0:T(8,128)(2,1)} %param.22) | copy-start | bytes 196612
  28.4 4.3 %copy-start.4 = (bf16[32,8,128]{2,1,0:T(8,128)(2,1)S(1)}, bf16[32,8,128]{2,1,0:T(8,128)(2,1)}, u32[]{:S(2)}) copy-start(bf16[32,8,128]{2,1,0:T(8,128)(2,1)} %param.23) | copy-start | bytes 196612
  28.4 4.3 %copy-start.5 = (bf16[4,32,2,32]{3,2,1,0:T(2,128)(2,1)S(1)}, bf16[4,32,2,32]{3,2,1,0:T(2,128)(2,1)}, u32[]{:S(2)}) copy-start(bf16[4,32,2,32]{3,2,1,0:T(2,128)(2,1)} %param.21) | copy-start | bytes 49156
  28.4 34.0 %copy-start.10 = (f32[1024,128]{1,0:T(8,128)S(1)}, f32[1024,128]{1,0:T(8,128)}, u32[]{:S(2)}) copy-start(f32[1024,128]{1,0:T(8,128)} %master_ref.1) | copy-start | bytes 1572868
  28.4 34.0 %copy-start.11 = (f32[1024,128]{1,0:T(8,128)S(1)}, f32[1024,128]{1,0:T(8,128)}, u32[]{:S(2)}) copy-start(f32[1024,128]{1,0:T(8,128)} %moment_ref.1) | copy-start | bytes 1572868
  29.3 33.2 %collective-permute-start.2 = (bf16[1024,128]{1,0:T(8,128)(2,1)}, bf16[1024,128]{1,0:T(8,128)(2,1)S(1)}, u32[]{:S(2)}, u32[]{:S(2)}) collective-permute-start(bf16[1024,128]{1,0:T(8,128)(2,1)} %pair_sum.1), channel_id=1, source_target_pairs={{0,64},{16,80},{32,96},{48,112},{64,0},{80,16},{96,32},{112,48},{1... | collective-permute-start | bytes 786440 | tf_op jit(solution)/shard_map/ppermute | solution.py:75
  51.0 15.9 %collective-permute-start.3 = (bf16[4,32,1024]{2,1,0:T(8,128)(2,1)S(1)}, bf16[4,32,1024]{2,1,0:T(8,128)(2,1)S(1)}, u32[]{:S(2)}, u32[]{:S(2)}) collective-permute-start(bf16[4,32,1024]{2,1,0:T(8,128)(2,1)S(1)} %all-to-all-done.same_ref), channel_id=1, source_target_pairs={{64,0},{80,16},{480,32},{496,48},{128,64},{144,80},{32,96},{48,112... | collective-permute-start | bytes 786440 | tf_op jit(solution)/shard_map/ppermute | solution.py:84
  53.1 13.9 %collective-permute-start.4 = (bf16[4,32,1024]{2,1,0:T(8,128)(2,1)S(1)}, bf16[4,32,1024]{2,1,0:T(8,128)(2,1)S(1)}, u32[]{:S(2)}, u32[]{:S(2)}) collective-permute-start(bf16[4,32,1024]{2,1,0:T(8,128)(2,1)S(1)} %all-to-all-done.same_ref), channel_id=1, source_target_pairs={{32,0},{48,16},{64,32},{80,48},{96,64},{112,80},{128,96},{144,112}... | collective-permute-start | bytes 786440 | tf_op jit(solution)/shard_map/ppermute | solution.py:84
  55.1 11.8 %collective-permute-start.5 = (bf16[4,32,1024]{2,1,0:T(8,128)(2,1)S(1)}, bf16[4,32,1024]{2,1,0:T(8,128)(2,1)S(1)}, u32[]{:S(2)}, u32[]{:S(2)}) collective-permute-start(bf16[4,32,1024]{2,1,0:T(8,128)(2,1)S(1)} %all-to-all-done.same_ref), channel_id=1, source_target_pairs={{480,0},{496,16},{0,32},{16,48},{32,64},{48,80},{64,96},{80,112},{... | collective-permute-start | bytes 786440 | tf_op jit(solution)/shard_map/ppermute | solution.py:84
  58.9 8.0 %collective-permute-start.6 = (bf16[784,128]{1,0:T(8,128)(2,1)S(1)}, bf16[784,128]{1,0:T(8,128)(2,1)S(1)}, u32[]{:S(2)}, u32[]{:S(2)}) collective-permute-start(bf16[784,128]{1,0:T(8,128)(2,1)S(1)} %pack_caches.1.refs_0_), channel_id=1, source_target_pairs={{0,1},{1,0},{2,3},{3,2},{4,5},{5,4},{6,7},{7,6},{8,9},{9,8},{10,11... | collective-permute-start | bytes 602120 | tf_op jit(solution)/shard_map/ppermute | solution.py:88
  66.9 28.0 %copy-start.6 = (bf16[4,32,256]{2,1,0:T(8,128)(2,1)S(1)}, bf16[4,32,256]{2,1,0:T(8,128)(2,1)}, u32[]{:S(2)}) copy-start(bf16[4,32,256]{2,1,0:T(8,128)(2,1)} %queries_ref.1) | copy-start | bytes 196612
  66.9 28.0 %copy-start.9 = (s32[32]{0:T(128)S(1)}, s32[32]{0:T(128)}, u32[]{:S(2)}) copy-start(s32[32]{0:T(128)} %param.25) | copy-start | bytes 388
  66.9 35.1 %copy-start.7 = (bf16[32,256]{1,0:T(8,128)(2,1)S(1)}, bf16[32,256]{1,0:T(8,128)(2,1)}, u32[]{:S(2)}) copy-start(bf16[32,256]{1,0:T(8,128)(2,1)} %state_ref.1) | copy-start | bytes 49156
  67.0 3.6 %collective-permute-start.7 = (bf16[1152,128]{1,0:T(8,128)(2,1)S(1)}, bf16[1152,128]{1,0:T(8,128)(2,1)S(1)}, u32[]{:S(2)}, u32[]{:S(2)}) collective-permute-start(bf16[1152,128]{1,0:T(8,128)(2,1)S(1)} %get-tuple-element.26.own_ref), channel_id=1, source_target_pairs={{0,16},{16,0},{32,48},{48,32},{64,80},{80,64},{96,112},{112,96},{1... | collective-permute-start | bytes 884744 | tf_op jit(solution)/shard_map/ppermute | solution.py:75
  72.5 15.1 %all-to-all-start.1 = ((bf16[16,2,32,128]{3,2,1,0:T(8,128)(2,1)}), bf16[16,2,32,128]{3,2,1,0:T(8,128)(2,1)S(1)}, u32[]{:S(2)}, u32[]{:S(2)}) async-start(bf16[16,2,32,128]{3,2,1,0:T(8,128)(2,1)} %project.1), calls=%async_computation.1 | async-start | bytes 524288 | tf_op jit(solution)/shard_map/all_to_all | solution.py:458
  79.7 15.2 %collective-permute-start.8 = (bf16[784,128]{1,0:T(8,128)(2,1)S(1)}, bf16[784,128]{1,0:T(8,128)(2,1)S(1)}, u32[]{:S(2)}, u32[]{:S(2)}) collective-permute-start(bf16[784,128]{1,0:T(8,128)(2,1)S(1)} %pack_caches.1.refs_0_), channel_id=1, source_target_pairs={{0,2},{1,3},{2,0},{3,1},{4,6},{5,7},{6,4},{7,5},{8,10},{9,11},{10,... | collective-permute-start | bytes 602120 | tf_op jit(solution)/shard_map/ppermute | solution.py:88
  84.6 10.4 %collective-permute-start.9 = (bf16[784,128]{1,0:T(8,128)(2,1)S(1)}, bf16[784,128]{1,0:T(8,128)(2,1)S(1)}, u32[]{:S(2)}, u32[]{:S(2)}) collective-permute-start(bf16[784,128]{1,0:T(8,128)(2,1)S(1)} %pack_caches.1.refs_0_), channel_id=1, source_target_pairs={{0,3},{1,2},{2,1},{3,0},{4,7},{5,6},{6,5},{7,4},{8,11},{9,10},{10,... | collective-permute-start | bytes 602120 | tf_op jit(solution)/shard_map/ppermute | solution.py:88
  87.7 14.3 %collective-permute-start.10 = (bf16[2,32,128]{2,1,0:T(8,128)(2,1)S(1)}, bf16[2,32,128]{2,1,0:T(8,128)(2,1)S(1)}, u32[]{:S(2)}, u32[]{:S(2)}) collective-permute-start(bf16[2,32,128]{2,1,0:T(8,128)(2,1)S(1)} %unit_sum.1), channel_id=1, source_target_pairs={{10,0},{11,32},{6,64},{13,96},{7,128},{2,160},{4,192},{1,224},{0,2... | collective-permute-start | bytes 49160 | tf_op jit(solution)/shard_map/ppermute | solution.py:459
  (6 other events, 9.9 us)

commit v5 on v4

--- a/solution.py
+++ b/solution.py
@@ -88,27 +88,35 @@
     return lax.ppermute(value, "tp", [(s, s ^ mask) for s in range(CHIPS)])
 
 
-def split_kernel(index_ref, grad_ref, out_ref):
+def chunk_at(j, dp, core):
+    return 2 * ((dp >> 1) ^ (((j & 1) << 1) | (j >> 1))) + core
+
+
+def split_kernel(dp_ref, grad_ref, out_ref):
     out_ref[0] = grad_ref[...]
 
 
-def take_chunks(index, grad):
+def take_chunks(dp, grad):
     return pl.pallas_call(
         split_kernel,
         grid_spec=pltpu.PrefetchScalarGridSpec(
             num_scalar_prefetch=1,
             grid=(4,),
-            in_specs=[pl.BlockSpec((UNITS, BLK), lambda j, index: (0, index[j]))],
-            out_specs=pl.BlockSpec((1, UNITS, BLK), lambda j, index: (j, 0, 0)),
+            in_specs=[
+                pl.BlockSpec(
+                    (UNITS, BLK), lambda j, dp: (0, chunk_at(j, dp[0], 1 - (dp[0] & 1)))
+                )
+            ],
+            out_specs=pl.BlockSpec((1, UNITS, BLK), lambda j, dp: (j, 0, 0)),
         ),
         out_shape=jax.ShapeDtypeStruct((4, UNITS, BLK), BF16),
         compiler_params=params(),
         name="take_chunks",
-    )(index, grad)
+    )(dp[None], grad)
 
 
 def core_sum_kernel(
-    index_ref, near_ref, far_ref, near_in_ref, far_in_ref, hidden_ref, keep_ref, send_ref, units_ref
+    dp_ref, near_ref, far_ref, near_in_ref, far_in_ref, hidden_ref, keep_ref, send_ref, units_ref
 ):
     keep_ref[0] = (near_ref[...].astype(F32) + near_in_ref[0].astype(F32)).astype(BF16)
     send_ref[0] = (far_ref[...].astype(F32) + far_in_ref[0].astype(F32)).astype(BF16)
@@ -123,8 +131,10 @@
             units_ref[run] = total
 
 
-def core_sum(index, grad, received, hidden):
-    whole = lambda shift: pl.BlockSpec((UNITS, BLK), lambda j, index: (0, index[j + shift]))
+def core_sum(dp, grad, received, hidden):
+    whole = lambda shift: pl.BlockSpec(
+        (UNITS, BLK), lambda j, dp: (0, chunk_at(j + shift, dp[0], dp[0] & 1))
+    )
     part = lambda shift: pl.BlockSpec((1, UNITS, BLK), lambda j, index: (j + shift, 0, 0))
     every = pl.BlockSpec(hidden.shape, lambda j, index: (0, 0, 0))
     shape = jax.ShapeDtypeStruct((2, UNITS, BLK), BF16)
@@ -139,7 +149,7 @@
         out_shape=[shape, shape, jax.ShapeDtypeStruct(hidden.shape, BF16)],
         compiler_params=params(),
         name="core_sum",
-    )(index, grad, grad, received, received, hidden)
+    )(dp[None], grad, grad, received, received, hidden)
 
 
 def pair_sum_kernel(keep_ref, received_ref, out_ref):
@@ -425,10 +435,9 @@
     plane = lax.axis_index("grp") * 4 + low
     grad = grad_partials[0]
 
-    owners = low ^ jnp.array([0, 2, 1, 3], jnp.int32)
-    outgoing = take_chunks(2 * owners + 1 - core, grad)
+    outgoing = take_chunks(dp, grad)
     received = flip(outgoing, 1)
-    keep, send, units = core_sum(2 * owners + core, grad, received, hidden)
+    keep, send, units = core_sum(dp, grad, received, hidden)
     second_in = flip(send, 2)
 
     same = lax.all_to_all(units, "grp", 0, 0)

time: 103 us -> 102 us (level)
    unnamed x34 -> x32, local copies, waits for them, and re-layouts: 4.82 us -> 4.82 us
where the time goes in v5:
time: 102 us; the launch traced here: 101 us
  starting transfers between devices  59 us (58%)
  waiting for transfers between devices  27.2 us (27%)
  Pallas kernels  8.14 us (8%)
  local copies, waits for them, and re-layouts  4.82 us (5%)
    all_to_all x1, waiting for transfers between devices, shards(): same = lax.all_to_all(units, 'grp', 0, 0)  18.2 us
    all_to_all x1, starting transfers between devices, shards(): same = lax.all_to_all(units, 'grp', 0, 0)  14.2 us
    ppermute x3, starting transfers between devices, swap(): return lax.ppermute(value, 'tp', [(s, s ^ mask) for s in range(CHIPS)])  11.4 us
    ppermute x4, starting transfers between devices, flip(): return lax.ppermute(value, 'dp', [(s, s ^ mask) for s in range(8)])  11.2 us
    ppermute x3, starting transfers between devices, from_plane(): return lax.ppermute(value, Z, pairs)  7.89 us
    ppermute x1, starting transfers between devices, shards(): mixed = lax.ppermute(unit_sum(parts), ALL, home_pairs())  7.17 us
    all_to_all x1, starting transfers between devices, shards(): parts = lax.all_to_all(parts, 'tp', 0, 0)  7.16 us
    ppermute x1, waiting for transfers between devices, shards(): mixed = lax.ppermute(unit_sum(parts), ALL, home_pairs())  5.64 us
  transfers between devices with their start and end apart: 13, of which 5 were waited for; matrix products, arithmetic and copies ran while one was open for 1% of the time, Pallas kernels for 4%

profile of v5, /device:TPU:4, one launch (start us, length us, event | category | flops | bytes accessed | tf_op | source)
XLA Modules:
  0.0 100.9 jit_solution(9490099768045779517)
XLA Ops:
  0.6 1.6 %copy-done = bf16[1,1024,1024]{2,1,0:T(8,128)(2,1)S(1)} copy-done((bf16[1,1024,1024]{2,1,0:T(8,128)(2,1)S(1)}, bf16[1,1024,1024]{2,1,0:T(8,128)(2,1)}, u32[]{:S(2)}) %copy-start) | copy-done | bytes 2097176
  2.7 1.9 %collective-permute-start = (bf16[4,1024,128]{2,1,0:T(8,128)(2,1)S(1)}, bf16[4,1024,128]{2,1,0:T(8,128)(2,1)S(1)}, u32[]{:S(2)}, u32[]{:S(2)}) collective-permute-start(bf16[4,1024,128]{2,1,0:T(8,128)(2,1)S(1)} %take_chunks.1), channel_id=1, source_target_pairs={{0,16},{16,0},{32,48},{48,32},{64,80},{80,64},{96,112},{112,96},{1... | collective-permute-start | bytes 3145736 | tf_op jit(solution)/shard_map/ppermute | solution.py:75
  4.6 2.6 %collective-permute-done.near_in_ref.far_in_ref = bf16[4,1024,128]{2,1,0:T(8,128)(2,1)S(1)} collective-permute-done((bf16[4,1024,128]{2,1,0:T(8,128)(2,1)S(1)}, bf16[4,1024,128]{2,1,0:T(8,128)(2,1)S(1)}, u32[]{:S(2)}, u32[]{:S(2)}) %collective-permute-start) | collective-permute-done | bytes 1048608 | tf_op jit(solution)/shard_map/ppermute | solution.py:75
  7.3 1.4 %core_sum.1 = (bf16[2,1024,128]{2,1,0:T(8,128)(2,1)S(1)}, bf16[2,1024,128]{2,1,0:T(8,128)(2,1)S(1)}, bf16[4,32,1024]{2,1,0:T(8,128)(2,1)}) custom-call(s32[1]{0:T(128)} %bitcast.dp_ref, bf16[1024,1024]{1,0:T(8,128)(2,1)S(1)} %bitcast.29, bf16[1024,1024]{1,0:T(8,128)(2,1)S(1)} %bitcast.30, ...), custom_call_target="tpu_custom_call" | custom-call | tf_op jit(solution)/shard_map/core_sum/pallas_call | solution.py:141
  8.6 3.8 %collective-permute-start.1 = (bf16[2,1024,128]{2,1,0:T(8,128)(2,1)S(1)}, bf16[2,1024,128]{2,1,0:T(8,128)(2,1)S(1)}, u32[]{:S(2)}, u32[]{:S(2)}) collective-permute-start(bf16[2,1024,128]{2,1,0:T(8,128)(2,1)S(1)} %get-tuple-element.17), channel_id=1, source_target_pairs={{0,32},{16,48},{32,0},{48,16},{64,96},{80,112},{96,64},{112,80},{1... | collective-permute-start | bytes 1572872 | tf_op jit(solution)/shard_map/ppermute | solution.py:75
  12.4 14.2 %all-to-all-start = ((bf16[4,32,1024]{2,1,0:T(8,128)(2,1)}), bf16[4,32,1024]{2,1,0:T(8,128)(2,1)S(1)}, u32[]{:S(2)}, u32[]{:S(2)}) async-start(bf16[4,32,1024]{2,1,0:T(8,128)(2,1)} %get-tuple-element.19), calls=%async_computation | async-start | bytes 524288 | tf_op jit(solution)/shard_map/all_to_all | solution.py:443
  27.5 3.4 %collective-permute-start.2 = (bf16[1024,128]{1,0:T(8,128)(2,1)}, bf16[1024,128]{1,0:T(8,128)(2,1)S(1)}, u32[]{:S(2)}, u32[]{:S(2)}) collective-permute-start(bf16[1024,128]{1,0:T(8,128)(2,1)} %pair_sum.1), channel_id=1, source_target_pairs={{0,64},{16,80},{32,96},{48,112},{64,0},{80,16},{96,32},{112,48},{1... | collective-permute-start | bytes 786440 | tf_op jit(solution)/shard_map/ppermute | solution.py:75
  31.1 18.2 %all-to-all-done.same_ref = bf16[4,32,1024]{2,1,0:T(8,128)(2,1)S(1)} async-done(((bf16[4,32,1024]{2,1,0:T(8,128)(2,1)}), bf16[4,32,1024]{2,1,0:T(8,128)(2,1)S(1)}, u32[]{:S(2)}, u32[]{:S(2)}) %all-to-all-start) | async-done | bytes 262176 | tf_op jit(solution)/shard_map/all_to_all | solution.py:443
  49.3 2.0 %collective-permute-start.3 = (bf16[4,32,1024]{2,1,0:T(8,128)(2,1)S(1)}, bf16[4,32,1024]{2,1,0:T(8,128)(2,1)S(1)}, u32[]{:S(2)}, u32[]{:S(2)}) collective-permute-start(bf16[4,32,1024]{2,1,0:T(8,128)(2,1)S(1)} %all-to-all-done.same_ref), channel_id=1, source_target_pairs={{64,0},{80,16},{480,32},{496,48},{128,64},{144,80},{32,96},{48,112... | collective-permute-start | bytes 786440 | tf_op jit(solution)/shard_map/ppermute | solution.py:84
  51.3 2.1 %collective-permute-start.4 = (bf16[4,32,1024]{2,1,0:T(8,128)(2,1)S(1)}, bf16[4,32,1024]{2,1,0:T(8,128)(2,1)S(1)}, u32[]{:S(2)}, u32[]{:S(2)}) collective-permute-start(bf16[4,32,1024]{2,1,0:T(8,128)(2,1)S(1)} %all-to-all-done.same_ref), channel_id=1, source_target_pairs={{32,0},{48,16},{64,32},{80,48},{96,64},{112,80},{128,96},{144,112}... | collective-permute-start | bytes 786440 | tf_op jit(solution)/shard_map/ppermute | solution.py:84
  53.4 3.8 %collective-permute-start.5 = (bf16[4,32,1024]{2,1,0:T(8,128)(2,1)S(1)}, bf16[4,32,1024]{2,1,0:T(8,128)(2,1)S(1)}, u32[]{:S(2)}, u32[]{:S(2)}) collective-permute-start(bf16[4,32,1024]{2,1,0:T(8,128)(2,1)S(1)} %all-to-all-done.same_ref), channel_id=1, source_target_pairs={{480,0},{496,16},{0,32},{16,48},{32,64},{48,80},{64,96},{80,112},{... | collective-permute-start | bytes 786440 | tf_op jit(solution)/shard_map/ppermute | solution.py:84
  57.2 3.5 %collective-permute-start.6 = (bf16[784,128]{1,0:T(8,128)(2,1)S(1)}, bf16[784,128]{1,0:T(8,128)(2,1)S(1)}, u32[]{:S(2)}, u32[]{:S(2)}) collective-permute-start(bf16[784,128]{1,0:T(8,128)(2,1)S(1)} %pack_caches.1.refs_0_), channel_id=1, source_target_pairs={{0,1},{1,0},{2,3},{3,2},{4,5},{5,4},{6,7},{7,6},{8,9},{9,8},{10,11... | collective-permute-start | bytes 602120 | tf_op jit(solution)/shard_map/ppermute | solution.py:88
  60.7 1.0 %copy-done.11 = f32[1024,128]{1,0:T(8,128)S(1)} copy-done((f32[1024,128]{1,0:T(8,128)S(1)}, f32[1024,128]{1,0:T(8,128)}, u32[]{:S(2)}) %copy-start.11) | copy-done | bytes 524312
  61.8 1.0 %copy-done.13 = bf16[2,1024,128]{2,1,0:T(8,128)(2,1)S(1)} copy-done((bf16[2,1024,128]{2,1,0:T(8,128)(2,1)S(1)}, bf16[2,1024,128]{2,1,0:T(8,128)(2,1)}, u32[]{:S(2)}) %copy-start.13) | copy-done | bytes 524312
  62.8 1.0 %copy-done.15 = bf16[2,1024,128]{2,1,0:T(8,128)(2,1)S(1)} copy-done((bf16[2,1024,128]{2,1,0:T(8,128)(2,1)S(1)}, bf16[2,1024,128]{2,1,0:T(8,128)(2,1)}, u32[]{:S(2)}) %copy-start.15) | copy-done | bytes 524312
  63.9 1.3 %update.1 = (bf16[1024,128]{1,0:T(8,128)(2,1)}, bf16[1152,128]{1,0:T(8,128)(2,1)S(1)}) custom-call(bf16[2,1024,128]{2,1,0:T(8,128)(2,1)S(1)} %copy-done.13, bf16[2,1024,128]{2,1,0:T(8,128)(2,1)S(1)} %copy-done.15, bf16[1024,128]{1,0:T(8,128)(2,1)S(1)} %collective-permute-done.2.third_in_ref, f32[1024,128]{1,0:T(8,128)S(1)} %copy-done.9, ...), custom_call_target="tpu_custom_call" | custom-call | flops 99999997952 | bytes 1000000000 | tf_op jit(solution)/shard_map/update/pallas_call | solution.py:207
  65.2 2.1 %collective-permute-start.7 = (bf16[1152,128]{1,0:T(8,128)(2,1)S(1)}, bf16[1152,128]{1,0:T(8,128)(2,1)S(1)}, u32[]{:S(2)}, u32[]{:S(2)}) collective-permute-start(bf16[1152,128]{1,0:T(8,128)(2,1)S(1)} %get-tuple-element.26.own_ref), channel_id=1, source_target_pairs={{0,16},{16,0},{32,48},{48,32},{64,80},{80,64},{96,112},{112,96},{1... | collective-permute-start | bytes 884744 | tf_op jit(solution)/shard_map/ppermute | solution.py:75
  68.8 2.0 %project.1 = bf16[16,2,32,128]{3,2,1,0:T(8,128)(2,1)} custom-call(s32[17]{0:T(128)S(1)} %pad_add_fusion.order_ref, bf16[4,32,1024]{2,1,0:T(8,128)(2,1)S(1)} %all-to-all-done.same_ref, bf16[4,32,1024]{2,1,0:T(8,128)(2,1)S(1)} %collective-permute-done.4.up_ref, bf16[4,32,1024]{2,1,0:T(8,128)(2,1)S(1)} %collective-permute-done.3.two_ref, ...), custom_call_target="tpu_custom_call" | custom-call | tf_op jit(solution)/shard_map/project/pallas_call | solution.py:247
  70.8 7.2 %all-to-all-start.1 = ((bf16[16,2,32,128]{3,2,1,0:T(8,128)(2,1)}), bf16[16,2,32,128]{3,2,1,0:T(8,128)(2,1)S(1)}, u32[]{:S(2)}, u32[]{:S(2)}) async-start(bf16[16,2,32,128]{3,2,1,0:T(8,128)(2,1)} %project.1), calls=%async_computation.1 | async-start | bytes 524288 | tf_op jit(solution)/shard_map/all_to_all | solution.py:467
  78.0 4.9 %collective-permute-start.8 = (bf16[784,128]{1,0:T(8,128)(2,1)S(1)}, bf16[784,128]{1,0:T(8,128)(2,1)S(1)}, u32[]{:S(2)}, u32[]{:S(2)}) collective-permute-start(bf16[784,128]{1,0:T(8,128)(2,1)S(1)} %pack_caches.1.refs_0_), channel_id=1, source_target_pairs={{0,2},{1,3},{2,0},{3,1},{4,6},{5,7},{6,4},{7,5},{8,10},{9,11},{10,... | collective-permute-start | bytes 602120 | tf_op jit(solution)/shard_map/ppermute | solution.py:88
  82.8 3.1 %collective-permute-start.9 = (bf16[784,128]{1,0:T(8,128)(2,1)S(1)}, bf16[784,128]{1,0:T(8,128)(2,1)S(1)}, u32[]{:S(2)}, u32[]{:S(2)}) collective-permute-start(bf16[784,128]{1,0:T(8,128)(2,1)S(1)} %pack_caches.1.refs_0_), channel_id=1, source_target_pairs={{0,3},{1,2},{2,1},{3,0},{4,7},{5,6},{6,5},{7,4},{8,11},{9,10},{10,... | collective-permute-start | bytes 602120 | tf_op jit(solution)/shard_map/ppermute | solution.py:88
  86.0 7.2 %collective-permute-start.10 = (bf16[2,32,128]{2,1,0:T(8,128)(2,1)S(1)}, bf16[2,32,128]{2,1,0:T(8,128)(2,1)S(1)}, u32[]{:S(2)}, u32[]{:S(2)}) collective-permute-start(bf16[2,32,128]{2,1,0:T(8,128)(2,1)S(1)} %unit_sum.1), channel_id=1, source_target_pairs={{10,0},{11,32},{6,64},{13,96},{7,128},{2,160},{4,192},{1,224},{0,2... | collective-permute-start | bytes 49160 | tf_op jit(solution)/shard_map/ppermute | solution.py:468
  93.2 1.5 %attend.1.attention_ref = f32[32,256]{1,0:T(8,128)S(1)} custom-call(s32[1]{0:T(128)} %bitcast.2.place_ref, s32[1,32]{1,0:T(1,128)S(1)} %bitcast.35, bf16[4,32,256]{2,1,0:T(8,128)(2,1)S(1)} %copy-done.5, bf16[784,128]{1,0:T(8,128)(2,1)S(1)} %pack_caches.1.refs_0_, bf16[784,128]{1,0:T(8,128)(2,1)S(1)} %collective-permute-done.6.refs_1_, ...), custom_call_target="tpu_custom_call" | custom-call | tf_op jit(solution)/shard_map/attend/pallas_call | solution.py:408
  94.7 5.6 %collective-permute-done.10.mixed_ref = bf16[2,32,128]{2,1,0:T(8,128)(2,1)S(1)} collective-permute-done((bf16[2,32,128]{2,1,0:T(8,128)(2,1)S(1)}, bf16[2,32,128]{2,1,0:T(8,128)(2,1)S(1)}, u32[]{:S(2)}, u32[]{:S(2)}) %collective-permute-start.10) | collective-permute-done | bytes 16416 | tf_op jit(solution)/shard_map/ppermute | solution.py:468
  (45 shorter events, 3.8 us)
Async XLA Ops:
  2.2 5.0 %copy-start.1 = (bf16[4,32,1024]{2,1,0:T(8,128)(2,1)S(1)}, bf16[4,32,1024]{2,1,0:T(8,128)(2,1)}, u32[]{:S(2)}) copy-start(bf16[4,32,1024]{2,1,0:T(8,128)(2,1)} %hidden_ref.1) | copy-start | bytes 786436
  2.7 4.6 %collective-permute-start = (bf16[4,1024,128]{2,1,0:T(8,128)(2,1)S(1)}, bf16[4,1024,128]{2,1,0:T(8,128)(2,1)S(1)}, u32[]{:S(2)}, u32[]{:S(2)}) collective-permute-start(bf16[4,1024,128]{2,1,0:T(8,128)(2,1)S(1)} %take_chunks.1), channel_id=1, source_target_pairs={{0,16},{16,0},{32,48},{48,32},{64,80},{80,64},{96,112},{112,96},{1... | collective-permute-start | bytes 3145736 | tf_op jit(solution)/shard_map/ppermute | solution.py:75
  8.6 18.9 %copy-start.12 = (bf16[2,1024,128]{2,1,0:T(8,128)(2,1)}, bf16[2,1024,128]{2,1,0:T(8,128)(2,1)S(1)}, u32[]{:S(2)}) copy-start(bf16[2,1024,128]{2,1,0:T(8,128)(2,1)S(1)} %get-tuple-element.16.keep_ref) | copy-start | bytes 1572868
  8.6 18.0 %collective-permute-start.1 = (bf16[2,1024,128]{2,1,0:T(8,128)(2,1)S(1)}, bf16[2,1024,128]{2,1,0:T(8,128)(2,1)S(1)}, u32[]{:S(2)}, u32[]{:S(2)}) collective-permute-start(bf16[2,1024,128]{2,1,0:T(8,128)(2,1)S(1)} %get-tuple-element.17), channel_id=1, source_target_pairs={{0,32},{16,48},{32,0},{48,16},{64,96},{80,112},{96,64},{112,80},{1... | collective-permute-start | bytes 1572872 | tf_op jit(solution)/shard_map/ppermute | solution.py:75
  12.4 36.8 %all-to-all-start = ((bf16[4,32,1024]{2,1,0:T(8,128)(2,1)}), bf16[4,32,1024]{2,1,0:T(8,128)(2,1)S(1)}, u32[]{:S(2)}, u32[]{:S(2)}) async-start(bf16[4,32,1024]{2,1,0:T(8,128)(2,1)} %get-tuple-element.19), calls=%async_computation | async-start | bytes 524288 | tf_op jit(solution)/shard_map/all_to_all | solution.py:443
  26.6 4.3 %copy-start.2 = (bf16[32,8,128]{2,1,0:T(8,128)(2,1)S(1)}, bf16[32,8,128]{2,1,0:T(8,128)(2,1)}, u32[]{:S(2)}) copy-start(bf16[32,8,128]{2,1,0:T(8,128)(2,1)} %param.21) | copy-start | bytes 196612
  26.7 4.3 %copy-start.3 = (bf16[32,8,128]{2,1,0:T(8,128)(2,1)S(1)}, bf16[32,8,128]{2,1,0:T(8,128)(2,1)}, u32[]{:S(2)}) copy-start(bf16[32,8,128]{2,1,0:T(8,128)(2,1)} %param.22) | copy-start | bytes 196612
  26.7 4.3 %copy-start.4 = (bf16[4,32,2,32]{3,2,1,0:T(2,128)(2,1)S(1)}, bf16[4,32,2,32]{3,2,1,0:T(2,128)(2,1)}, u32[]{:S(2)}) copy-start(bf16[4,32,2,32]{3,2,1,0:T(2,128)(2,1)} %param.20) | copy-start | bytes 49156
  26.7 4.3 %copy-start.7 = (bf16[32,2,8]{0,2,1:T(8,128)(2,1)S(1)}, bf16[32,2,8]{0,2,1:T(8,128)(2,1)}, u32[]{:S(2)}) copy-start(bf16[32,2,8]{0,2,1:T(8,128)(2,1)} %param.23) | copy-start | bytes 3076
  26.7 34.0 %copy-start.9 = (f32[1024,128]{1,0:T(8,128)S(1)}, f32[1024,128]{1,0:T(8,128)}, u32[]{:S(2)}) copy-start(f32[1024,128]{1,0:T(8,128)} %master_ref.1) | copy-start | bytes 1572868
  26.7 34.0 %copy-start.10 = (f32[1024,128]{1,0:T(8,128)S(1)}, f32[1024,128]{1,0:T(8,128)}, u32[]{:S(2)}) copy-start(f32[1024,128]{1,0:T(8,128)} %moment_ref.1) | copy-start | bytes 1572868
  27.5 33.1 %collective-permute-start.2 = (bf16[1024,128]{1,0:T(8,128)(2,1)}, bf16[1024,128]{1,0:T(8,128)(2,1)S(1)}, u32[]{:S(2)}, u32[]{:S(2)}) collective-permute-start(bf16[1024,128]{1,0:T(8,128)(2,1)} %pair_sum.1), channel_id=1, source_target_pairs={{0,64},{16,80},{32,96},{48,112},{64,0},{80,16},{96,32},{112,48},{1... | collective-permute-start | bytes 786440 | tf_op jit(solution)/shard_map/ppermute | solution.py:75
  49.3 15.9 %collective-permute-start.3 = (bf16[4,32,1024]{2,1,0:T(8,128)(2,1)S(1)}, bf16[4,32,1024]{2,1,0:T(8,128)(2,1)S(1)}, u32[]{:S(2)}, u32[]{:S(2)}) collective-permute-start(bf16[4,32,1024]{2,1,0:T(8,128)(2,1)S(1)} %all-to-all-done.same_ref), channel_id=1, source_target_pairs={{64,0},{80,16},{480,32},{496,48},{128,64},{144,80},{32,96},{48,112... | collective-permute-start | bytes 786440 | tf_op jit(solution)/shard_map/ppermute | solution.py:84
  51.3 13.9 %collective-permute-start.4 = (bf16[4,32,1024]{2,1,0:T(8,128)(2,1)S(1)}, bf16[4,32,1024]{2,1,0:T(8,128)(2,1)S(1)}, u32[]{:S(2)}, u32[]{:S(2)}) collective-permute-start(bf16[4,32,1024]{2,1,0:T(8,128)(2,1)S(1)} %all-to-all-done.same_ref), channel_id=1, source_target_pairs={{32,0},{48,16},{64,32},{80,48},{96,64},{112,80},{128,96},{144,112}... | collective-permute-start | bytes 786440 | tf_op jit(solution)/shard_map/ppermute | solution.py:84
  53.4 11.8 %collective-permute-start.5 = (bf16[4,32,1024]{2,1,0:T(8,128)(2,1)S(1)}, bf16[4,32,1024]{2,1,0:T(8,128)(2,1)S(1)}, u32[]{:S(2)}, u32[]{:S(2)}) collective-permute-start(bf16[4,32,1024]{2,1,0:T(8,128)(2,1)S(1)} %all-to-all-done.same_ref), channel_id=1, source_target_pairs={{480,0},{496,16},{0,32},{16,48},{32,64},{48,80},{64,96},{80,112},{... | collective-permute-start | bytes 786440 | tf_op jit(solution)/shard_map/ppermute | solution.py:84
  57.2 8.0 %collective-permute-start.6 = (bf16[784,128]{1,0:T(8,128)(2,1)S(1)}, bf16[784,128]{1,0:T(8,128)(2,1)S(1)}, u32[]{:S(2)}, u32[]{:S(2)}) collective-permute-start(bf16[784,128]{1,0:T(8,128)(2,1)S(1)} %pack_caches.1.refs_0_), channel_id=1, source_target_pairs={{0,1},{1,0},{2,3},{3,2},{4,5},{5,4},{6,7},{7,6},{8,9},{9,8},{10,11... | collective-permute-start | bytes 602120 | tf_op jit(solution)/shard_map/ppermute | solution.py:88
  65.2 28.0 %copy-start.5 = (bf16[4,32,256]{2,1,0:T(8,128)(2,1)S(1)}, bf16[4,32,256]{2,1,0:T(8,128)(2,1)}, u32[]{:S(2)}) copy-start(bf16[4,32,256]{2,1,0:T(8,128)(2,1)} %queries_ref.1) | copy-start | bytes 196612
  65.2 28.0 %copy-start.8 = (s32[32]{0:T(128)S(1)}, s32[32]{0:T(128)}, u32[]{:S(2)}) copy-start(s32[32]{0:T(128)} %param.24) | copy-start | bytes 388
  65.2 35.1 %copy-start.6 = (bf16[32,256]{1,0:T(8,128)(2,1)S(1)}, bf16[32,256]{1,0:T(8,128)(2,1)}, u32[]{:S(2)}) copy-start(bf16[32,256]{1,0:T(8,128)(2,1)} %state_ref.1) | copy-start | bytes 49156
  65.2 3.6 %collective-permute-start.7 = (bf16[1152,128]{1,0:T(8,128)(2,1)S(1)}, bf16[1152,128]{1,0:T(8,128)(2,1)S(1)}, u32[]{:S(2)}, u32[]{:S(2)}) collective-permute-start(bf16[1152,128]{1,0:T(8,128)(2,1)S(1)} %get-tuple-element.26.own_ref), channel_id=1, source_target_pairs={{0,16},{16,0},{32,48},{48,32},{64,80},{80,64},{96,112},{112,96},{1... | collective-permute-start | bytes 884744 | tf_op jit(solution)/shard_map/ppermute | solution.py:75
  70.8 15.1 %all-to-all-start.1 = ((bf16[16,2,32,128]{3,2,1,0:T(8,128)(2,1)}), bf16[16,2,32,128]{3,2,1,0:T(8,128)(2,1)S(1)}, u32[]{:S(2)}, u32[]{:S(2)}) async-start(bf16[16,2,32,128]{3,2,1,0:T(8,128)(2,1)} %project.1), calls=%async_computation.1 | async-start | bytes 524288 | tf_op jit(solution)/shard_map/all_to_all | solution.py:467
  78.0 15.2 %collective-permute-start.8 = (bf16[784,128]{1,0:T(8,128)(2,1)S(1)}, bf16[784,128]{1,0:T(8,128)(2,1)S(1)}, u32[]{:S(2)}, u32[]{:S(2)}) collective-permute-start(bf16[784,128]{1,0:T(8,128)(2,1)S(1)} %pack_caches.1.refs_0_), channel_id=1, source_target_pairs={{0,2},{1,3},{2,0},{3,1},{4,6},{5,7},{6,4},{7,5},{8,10},{9,11},{10,... | collective-permute-start | bytes 602120 | tf_op jit(solution)/shard_map/ppermute | solution.py:88
  82.8 10.4 %collective-permute-start.9 = (bf16[784,128]{1,0:T(8,128)(2,1)S(1)}, bf16[784,128]{1,0:T(8,128)(2,1)S(1)}, u32[]{:S(2)}, u32[]{:S(2)}) collective-permute-start(bf16[784,128]{1,0:T(8,128)(2,1)S(1)} %pack_caches.1.refs_0_), channel_id=1, source_target_pairs={{0,3},{1,2},{2,1},{3,0},{4,7},{5,6},{6,5},{7,4},{8,11},{9,10},{10,... | collective-permute-start | bytes 602120 | tf_op jit(solution)/shard_map/ppermute | solution.py:88
  86.0 14.3 %collective-permute-start.10 = (bf16[2,32,128]{2,1,0:T(8,128)(2,1)S(1)}, bf16[2,32,128]{2,1,0:T(8,128)(2,1)S(1)}, u32[]{:S(2)}, u32[]{:S(2)}) collective-permute-start(bf16[2,32,128]{2,1,0:T(8,128)(2,1)S(1)} %unit_sum.1), channel_id=1, source_target_pairs={{10,0},{11,32},{6,64},{13,96},{7,128},{2,160},{4,192},{1,224},{0,2... | collective-permute-start | bytes 49160 | tf_op jit(solution)/shard_map/ppermute | solution.py:468
  (5 other events, 5.6 us)
